TPU v7x, 32 devices: a whole 2x2x4 slice. The times are simulated.
32 devices in a mesh: gx: 8 (over y, x, core), gy: 4 (over z).
Axes of the slice: x: 2, y: 2, z: 4, core: 2. Of those that a mesh axis runs over, the one named last changes fastest.
Arguments:
- mass_per_volume: float32 [64, 32, 128], P('gx', 'gy'), may hold values from 0.4 to 2.5
- velocity: float32 [3, 64, 32, 128], P(None, 'gx', 'gy'), may hold values from -3 to 3
- thermal_stress: float32 [64, 32, 128], P('gx', 'gy'), may hold values from 0.06 to 1.5
- magnetic: float32 [3, 64, 32, 128], P(None, 'gx', 'gy'), may hold values from -4.8 to 4.8, as said below
Outputs:
- density_out: float32 [64, 32, 128], P('gx', 'gy')
- velocity_out: float32 [3, 64, 32, 128], P(None, 'gx', 'gy')
- pressure_out: float32 [64, 32, 128], P('gx', 'gy')
- magnetic_out: float32 [3, 64, 32, 128], P(None, 'gx', 'gy')
Inputs may be any that keep to these rules, and one draw needn't show every extreme that they name: magnetic has zero discrete divergence in every cell: the sum over c of b_c at i+1 minus b_c at i along c vanishes up to rounding.
All inputs are finite; a program needn't handle non-finite values.
Results may differ from a plain program's by a relative error of at most 0.0003.
Values sent between devices are 32-bit elements; how exact they have to be, the bound alone decides.
A program may use at most 128 MiB of HBM per device.

v0:
```python
import jax
import jax.numpy as jnp
from jax import lax
from jax.sharding import PartitionSpec as P

SECTIONS = 4
SUPER_SECTIONS = 8


GAMMA_RATIO = 5.0 / 3.0
TIME_STEP = 0.04
SUPER_TIME = 0.08
DENSITY_FLOOR = 0.5
PRESSURE_FLOOR = 0.1
FIELD_FLOOR = 0.05


def extended_2(block, sides, width):
    for axis, dim in sides:
        count = lax.axis_size(axis)
        forward = [(i, i + 1) for i in range(count - 1)]
        forward.append((count - 1, 0))
        backward = [(target, source) for source, target in forward]
        low = lax.ppermute(
            lax.slice_in_dim(block, block.shape[dim] - width, None, axis=dim), axis, forward
        )
        high = lax.ppermute(lax.slice_in_dim(block, 0, width, axis=dim), axis, backward)
        block = jnp.concatenate([low, block, high], axis=dim)
    return block


def adjacent_zone(a, dimension, k):
    return jnp.roll(a, -k, dimension)


def minmod(lower, upper):
    return 0.5 * (jnp.sign(lower) + jnp.sign(upper)) * jnp.minimum(jnp.abs(lower), jnp.abs(upper))


def wave_fluxes(mass_per_volume, velocity, thermal_stress, magnetic, adjacent_quantities):
    magnetic_sq = magnetic[0] * magnetic[0] + magnetic[1] * magnetic[1] + magnetic[2] * magnetic[2]
    kinetic = velocity[0] * velocity[0] + velocity[1] * velocity[1] + velocity[2] * velocity[2]
    whole_work_content = (
        thermal_stress / (GAMMA_RATIO - 1.0) + 0.5 * mass_per_volume * kinetic + 0.5 * magnetic_sq
    )
    pressure_total = thermal_stress + 0.5 * magnetic_sq
    normal_speed = velocity[adjacent_quantities]
    normal_field = magnetic[adjacent_quantities]
    projection = velocity[0] * magnetic[0] + velocity[1] * magnetic[1] + velocity[2] * magnetic[2]
    others = [
        zone_quantities for zone_quantities in range(3) if zone_quantities != adjacent_quantities
    ]
    conserved = (
        [mass_per_volume]
        + [mass_per_volume * velocity[zone_quantities] for zone_quantities in range(3)]
        + [whole_work_content]
        + [magnetic[zone_quantities] for zone_quantities in others]
    )
    momentum_fluxes = []
    for zone_quantities in range(3):
        momentum_term = (
            mass_per_volume * normal_speed * velocity[zone_quantities]
            - normal_field * magnetic[zone_quantities]
        )
        if zone_quantities == adjacent_quantities:
            momentum_term = momentum_term + pressure_total
        momentum_fluxes.append(momentum_term)
    fluxes = [mass_per_volume * normal_speed] + momentum_fluxes
    fluxes = fluxes + [
        (whole_work_content + pressure_total) * normal_speed - normal_field * projection
    ]
    fluxes = fluxes + [
        normal_speed * magnetic[zone_quantities] - velocity[zone_quantities] * normal_field
        for zone_quantities in others
    ]
    signal = jnp.abs(normal_speed) + jnp.sqrt(
        (GAMMA_RATIO * thermal_stress + magnetic_sq) / mass_per_volume
    )
    return (conserved, fluxes, signal)


def face_fluxes(
    mass_per_volume, velocity, thermal_stress, cell_field, face_field, adjacent_quantities
):
    primitive = [mass_per_volume] + list(velocity) + [thermal_stress] + list(cell_field)
    lower_states = []
    upper_states = []
    for n in range(8):
        if n == 5 + adjacent_quantities:
            lower_states.append(face_field[adjacent_quantities])
            upper_states.append(face_field[adjacent_quantities])
        else:
            quantity = primitive[n]
            gradient = minmod(
                quantity - adjacent_zone(quantity, adjacent_quantities, -1),
                adjacent_zone(quantity, adjacent_quantities, 1) - quantity,
            )
            lower_states.append(adjacent_zone(quantity + 0.5 * gradient, adjacent_quantities, -1))
            upper_states.append(quantity - 0.5 * gradient)
    conserved_lower, flux_lower, signal_lower = wave_fluxes(
        lower_states[0], lower_states[1:4], lower_states[4], lower_states[5:8], adjacent_quantities
    )
    conserved_upper, flux_upper, signal_upper = wave_fluxes(
        upper_states[0], upper_states[1:4], upper_states[4], upper_states[5:8], adjacent_quantities
    )
    signal = jnp.maximum(signal_lower, signal_upper)
    return [
        0.5 * (flux_lower[n] + flux_upper[n])
        - 0.5 * signal * (conserved_upper[n] - conserved_lower[n])
        for n in range(7)
    ]


def hyperbolic(mass_per_volume, velocity, thermal_stress, face_field):
    cell_field = [
        0.5
        * (
            face_field[zone_quantities]
            + adjacent_zone(face_field[zone_quantities], zone_quantities, 1)
        )
        for zone_quantities in range(3)
    ]
    momentum = [mass_per_volume * velocity[zone_quantities] for zone_quantities in range(3)]
    kinetic = velocity[0] * velocity[0] + velocity[1] * velocity[1] + velocity[2] * velocity[2]
    magnetic_sq = (
        cell_field[0] * cell_field[0]
        + cell_field[1] * cell_field[1]
        + cell_field[2] * cell_field[2]
    )
    whole_work_content = (
        thermal_stress / (GAMMA_RATIO - 1.0) + 0.5 * mass_per_volume * kinetic + 0.5 * magnetic_sq
    )
    conserved = [mass_per_volume] + momentum + [whole_work_content]
    directional = [
        face_fluxes(
            mass_per_volume, velocity, thermal_stress, cell_field, face_field, adjacent_quantities
        )
        for adjacent_quantities in range(3)
    ]
    updated = []
    for n in range(5):
        change = conserved[n]
        for adjacent_quantities in range(3):
            change = change - TIME_STEP * (
                adjacent_zone(directional[adjacent_quantities][n], adjacent_quantities, 1)
                - directional[adjacent_quantities][n]
            )
        updated.append(change)

    def induction(adjacent_quantities, zone_quantities):
        others = [e for e in range(3) if e != adjacent_quantities]
        return directional[adjacent_quantities][5 + others.index(zone_quantities)]

    x_flux_y = induction(0, 1)
    y_flux_x = induction(1, 0)
    x_flux_z = induction(0, 2)
    z_flux_x = induction(2, 0)
    y_flux_z = induction(1, 2)
    z_flux_y = induction(2, 1)
    edge_z = 0.25 * (
        adjacent_zone(y_flux_x, 0, -1) + y_flux_x - adjacent_zone(x_flux_y, 1, -1) - x_flux_y
    )
    edge_y = 0.25 * (
        adjacent_zone(x_flux_z, 2, -1) + x_flux_z - adjacent_zone(z_flux_x, 0, -1) - z_flux_x
    )
    edge_x = 0.25 * (
        adjacent_zone(z_flux_y, 1, -1) + z_flux_y - adjacent_zone(y_flux_z, 2, -1) - y_flux_z
    )
    new_face = [
        face_field[0]
        - TIME_STEP * (adjacent_zone(edge_z, 1, 1) - edge_z)
        + TIME_STEP * (adjacent_zone(edge_y, 2, 1) - edge_y),
        face_field[1]
        - TIME_STEP * (adjacent_zone(edge_x, 2, 1) - edge_x)
        + TIME_STEP * (adjacent_zone(edge_z, 0, 1) - edge_z),
        face_field[2]
        - TIME_STEP * (adjacent_zone(edge_y, 0, 1) - edge_y)
        + TIME_STEP * (adjacent_zone(edge_x, 1, 1) - edge_x),
    ]
    floored = jnp.maximum(updated[0], DENSITY_FLOOR)
    new_velocity = [updated[1 + zone_quantities] / floored for zone_quantities in range(3)]
    new_cell = [
        0.5
        * (new_face[zone_quantities] + adjacent_zone(new_face[zone_quantities], zone_quantities, 1))
        for zone_quantities in range(3)
    ]
    kinetic_new = (
        updated[1] * new_velocity[0] + updated[2] * new_velocity[1] + updated[3] * new_velocity[2]
    )
    magnetic_new = new_cell[0] * new_cell[0] + new_cell[1] * new_cell[1] + new_cell[2] * new_cell[2]
    internal = updated[4] - 0.5 * kinetic_new - 0.5 * magnetic_new
    new_pressure = jnp.maximum((GAMMA_RATIO - 1.0) * internal, PRESSURE_FLOOR)
    return (floored, new_velocity, new_pressure, new_face)


def coefficients(mass_per_volume, thermal_stress, face_field):
    plasma_thermal_level = thermal_stress / mass_per_volume
    thermal_diffusion_coefficient = (
        plasma_thermal_level * plasma_thermal_level * jnp.sqrt(plasma_thermal_level)
    )
    cell_field = [
        0.5
        * (
            face_field[zone_quantities]
            + adjacent_zone(face_field[zone_quantities], zone_quantities, 1)
        )
        for zone_quantities in range(3)
    ]
    coupling = []
    for adjacent_quantities in range(3):
        components = []
        for zone_quantities in range(3):
            if zone_quantities == adjacent_quantities:
                components.append(face_field[adjacent_quantities])
            else:
                components.append(
                    0.5
                    * (
                        cell_field[zone_quantities]
                        + adjacent_zone(cell_field[zone_quantities], adjacent_quantities, -1)
                    )
                )
        magnitude = (
            components[0] * components[0]
            + components[1] * components[1]
            + components[2] * components[2]
        )
        factor = (
            0.5
            * (
                thermal_diffusion_coefficient
                + adjacent_zone(thermal_diffusion_coefficient, adjacent_quantities, -1)
            )
            / jnp.maximum(magnitude, FIELD_FLOOR)
        )
        coupling.append(
            [
                factor * face_field[adjacent_quantities] * components[zone_quantities]
                for zone_quantities in range(3)
            ]
        )
    return coupling


def conduction(whole_work_content, mass_per_volume, coupling):
    plasma_thermal_level = (GAMMA_RATIO - 1.0) * whole_work_content / mass_per_volume
    middle_derivative = [
        0.5
        * (
            adjacent_zone(plasma_thermal_level, zone_quantities, 1)
            - adjacent_zone(plasma_thermal_level, zone_quantities, -1)
        )
        for zone_quantities in range(3)
    ]
    result = jnp.zeros_like(whole_work_content)
    for adjacent_quantities in range(3):
        clipped_derivatives = []
        for zone_quantities in range(3):
            if zone_quantities == adjacent_quantities:
                clipped_derivatives.append(
                    plasma_thermal_level
                    - adjacent_zone(plasma_thermal_level, adjacent_quantities, -1)
                )
            else:
                clipped_derivatives.append(
                    0.5
                    * (
                        middle_derivative[zone_quantities]
                        + adjacent_zone(middle_derivative[zone_quantities], adjacent_quantities, -1)
                    )
                )
        heat_flux = -(
            coupling[adjacent_quantities][0] * clipped_derivatives[0]
            + coupling[adjacent_quantities][1] * clipped_derivatives[1]
            + coupling[adjacent_quantities][2] * clipped_derivatives[2]
        )
        result = result - (adjacent_zone(heat_flux, adjacent_quantities, 1) - heat_flux)
    return result


def super_step(whole_work_content, initial_rate, operator):
    b = [1.0 / 3.0, 1.0 / 3.0, 1.0 / 3.0] + [
        (j * j + j - 2.0) / (2.0 * j * (j + 1.0)) for j in range(3, SUPER_SECTIONS + 1)
    ]
    base_rate = 4.0 / (SUPER_SECTIONS * SUPER_SECTIONS + SUPER_SECTIONS - 2.0)
    earlier = whole_work_content
    latest = whole_work_content + b[1] * base_rate * SUPER_TIME * initial_rate
    for j in range(2, SECTIONS + 1):
        factor_prev = (2.0 * j - 1.0) / j * b[j] / b[j - 1]
        factor_back = -(j - 1.0) / j * b[j] / b[j - 2]
        factor_rate = factor_prev * base_rate
        factor_zero = -(1.0 - b[j - 1]) * factor_rate
        advanced = (
            factor_prev * latest
            + factor_back * earlier
            + (1.0 - factor_prev - factor_back) * whole_work_content
            + factor_rate * SUPER_TIME * operator(latest)
            + factor_zero * SUPER_TIME * initial_rate
        )
        earlier = latest
        latest = advanced
    return latest


def interior(a, margin):
    return a[margin : a.shape[0] - margin, margin : a.shape[1] - margin]


def local(mass_per_volume, velocity, thermal_stress, magnetic):
    stacked = jnp.concatenate(
        [mass_per_volume[None], velocity, thermal_stress[None], magnetic], axis=0
    )
    extended = extended_2(stacked, (("gx", 1), ("gy", 2)), 3)
    new_density, new_velocity, new_pressure, new_face = hyperbolic(
        extended[0],
        [extended[1], extended[2], extended[3]],
        extended[4],
        [extended[5], extended[6], extended[7]],
    )
    inner_density = interior(new_density, 3)
    inner_velocity = [interior(a, 3) for a in new_velocity]
    inner_face = [interior(a, 3) for a in new_face]
    heat_input = jnp.stack([inner_density, interior(new_pressure, 3)] + inner_face)
    beside_all = extended_2(heat_input, (("gx", 1), ("gy", 2)), 1)
    coupling = coefficients(
        beside_all[0], beside_all[1], [beside_all[2], beside_all[3], beside_all[4]]
    )
    energy_ext = beside_all[1] / (GAMMA_RATIO - 1.0)
    initial_rate = interior(conduction(energy_ext, beside_all[0], coupling), 1)

    def operator(whole_work_content):
        rimmed = extended_2(whole_work_content, (("gx", 0), ("gy", 1)), 1)
        return interior(conduction(rimmed, beside_all[0], coupling), 1)

    closing = super_step(interior(energy_ext, 1), initial_rate, operator)
    result = jnp.stack(
        [inner_density] + inner_velocity + [(GAMMA_RATIO - 1.0) * closing] + inner_face
    )
    return (result[0], result[1:4], result[4], result[5:8])


def solution(mesh):
    placed = (
        P("gx", "gy", None),
        P(None, "gx", "gy", None),
        P("gx", "gy", None),
        P(None, "gx", "gy", None),
    )
    return jax.shard_map(
        local,
        mesh=mesh,
        in_specs=placed,
        out_specs=(
            P("gx", "gy", None),
            P(None, "gx", "gy", None),
            P("gx", "gy", None),
            P(None, "gx", "gy", None),
        ),
        check_vma=False,
    )
```

profile of v0, /device:TPU:0, one launch (start us, length us, event | category | flops | bytes accessed | tf_op | source)
XLA Modules:
  0.0 92.0 jit_solution(371065047267782404)
XLA Ops:
  0.7 0.9 %pad_maximum_fusion.27 = (f32[8,3,8,128]{3,2,1,0:T(8,128)S(1)}, f32[8,3,8,128]{3,2,1,0:T(8,128)S(1)}) fusion(f32[3,8,8,128]{3,2,1,0:T(8,128)} %param.7, f32[1,8,8,128]{3,2,1,0:T(8,128)} %bitcast.445, f32[3,8,8,128]{3,2,1,0:T(8,128)} %param.5, f32[1,8,8,128]{3,2,1,0:T(8,128)} %bitcast.448), kind=kLoop, calls=%fused_computation.296 | loop fusion | flops 147456 | bytes 458752 | tf_op jit(solution)/shard_map/slice | solution.py:25
  2.1 2.9 %collective-permute-start.1 = (f32[8,3,8,128]{3,2,1,0:T(8,128)S(1)}, f32[8,3,8,128]{3,2,1,0:T(8,128)S(1)}, u32[]{:S(2)}, u32[]{:S(2)}) collective-permute-start(f32[8,3,8,128]{3,2,1,0:T(8,128)S(1)} %get-tuple-element.137), channel_id=1, source_target_pairs={{4,0},{8,4},{12,8},{16,12},{20,16},{24,20},{28,24},{0,28},{5,1},{9... | collective-permute-start | bytes 294920 | tf_op jit(solution)/shard_map/ppermute | solution.py:27
  5.1 2.2 %collective-permute-done = f32[8,3,8,128]{3,2,1,0:T(8,128)S(1)} collective-permute-done((f32[8,3,8,128]{3,2,1,0:T(8,128)S(1)}, f32[8,3,8,128]{3,2,1,0:T(8,128)S(1)}, u32[]{:S(2)}, u32[]{:S(2)}) %collective-permute-start) | collective-permute-done | bytes 98336 | tf_op jit(solution)/shard_map/ppermute | solution.py:24
  7.5 2.4 %collective-permute-start.2 = (f32[8,14,3,128]{3,2,1,0:T(4,128)S(1)}, f32[8,14,3,128]{3,2,1,0:T(4,128)S(1)}, u32[]{:S(2)}, u32[]{:S(2)}) collective-permute-start(f32[8,14,3,128]{3,2,1,0:T(4,128)S(1)} %get-tuple-element.125), channel_id=1, source_target_pairs={{0,1},{1,2},{2,3},{3,0},{4,5},{5,6},{6,7},{7,4},{8,9},{9,10},{10,1... | collective-permute-start | bytes 516104 | tf_op jit(solution)/shard_map/ppermute | solution.py:24
  9.8 2.1 %collective-permute-start.3 = (f32[8,14,3,128]{3,2,1,0:T(4,128)S(1)}, f32[8,14,3,128]{3,2,1,0:T(4,128)S(1)}, u32[]{:S(2)}, u32[]{:S(2)}) collective-permute-start(f32[8,14,3,128]{3,2,1,0:T(4,128)S(1)} %get-tuple-element.126), channel_id=1, source_target_pairs={{1,0},{2,1},{3,2},{0,3},{5,4},{6,5},{7,6},{4,7},{9,8},{10,9},{11,1... | collective-permute-start | bytes 516104 | tf_op jit(solution)/shard_map/ppermute | solution.py:27
  11.9 6.3 %collective-permute-done.2 = f32[8,14,3,128]{3,2,1,0:T(4,128)S(1)} collective-permute-done((f32[8,14,3,128]{3,2,1,0:T(4,128)S(1)}, f32[8,14,3,128]{3,2,1,0:T(4,128)S(1)}, u32[]{:S(2)}, u32[]{:S(2)}) %collective-permute-start.2) | collective-permute-done | bytes 172064 | tf_op jit(solution)/shard_map/ppermute | solution.py:24
  18.2 4.7 %collective-permute-done.3 = f32[8,14,3,128]{3,2,1,0:T(4,128)S(1)} collective-permute-done((f32[8,14,3,128]{3,2,1,0:T(4,128)S(1)}, f32[8,14,3,128]{3,2,1,0:T(4,128)S(1)}, u32[]{:S(2)}, u32[]{:S(2)}) %collective-permute-start.3) | collective-permute-done | bytes 172064 | tf_op jit(solution)/shard_map/ppermute | solution.py:27
  26.1 1.1 %multiply_subtract_fusion.8 = (f32[14,14,128]{2,1,0:T(8,128)S(1)}, f32[14,14,128]{2,1,0:T(8,128)S(1)}, f32[14,14,128]{2,1,0:T(8,128)S(1)}, f32[14,14,128]{2,1,0:...) fusion(f32[13,14,128]{2,1,0:T(8,128)S(1)} %slice.1861, ...), kind=kLoop, calls=%fused_computation.170 | loop fusion | flops 4340224 | bytes 3813376 | tf_op jit(solution)/shard_map/sub | solution.py:108
  29.5 1.3 %multiply_subtract_fusion.7 = (f32[14,14,128]{2,1,0:T(8,128)S(1)}, f32[14,14,128]{2,1,0:T(8,128)S(1)}, f32[14,14,128]{2,1,0:T(8,128)S(1)}, f32[14,14,128]{2,1,0:...) fusion(f32[14,13,128]{2,1,0:T(8,128)S(1)} %bitcast.412, ...), kind=kLoop, calls=%fused_computation.169 | loop fusion | flops 4340224 | bytes 3813376 | tf_op jit(solution)/shard_map/sub | solution.py:108
  33.8 1.4 %multiply_subtract_fusion.6 = (f32[14,14,128]{2,1,0:T(8,128)S(1)}, f32[14,14,128]{2,1,0:T(8,128)S(1)}, f32[14,14,128]{2,1,0:T(8,128)S(1)}, f32[14,14,128]{2,1,0:...) fusion(f32[14,14,127]{2,1,0:T(8,128)S(1)} %bitcast.418, ...), kind=kLoop, calls=%fused_computation.168 | loop fusion | flops 4340224 | bytes 4214784 | tf_op jit(solution)/shard_map/sub | solution.py:108
  38.1 0.8 copy-done.7
  40.6 2.6 %collective-permute-start.5 = (f32[5,1,8,128]{3,2,1,0:T(8,128)S(1)}, f32[5,1,8,128]{3,2,1,0:T(8,128)S(1)}, u32[]{:S(2)}, u32[]{:S(2)}) collective-permute-start(f32[5,1,8,128]{3,2,1,0:T(8,128)S(1)} %get-tuple-element.147), channel_id=1, source_target_pairs={{4,0},{8,4},{12,8},{16,12},{20,16},{24,20},{28,24},{0,28},{5,1},{9... | collective-permute-start | bytes 61448 | tf_op jit(solution)/shard_map/ppermute | solution.py:27
  43.2 1.5 %collective-permute-done.4 = f32[5,1,8,128]{3,2,1,0:T(8,128)S(1)} collective-permute-done((f32[5,1,8,128]{3,2,1,0:T(8,128)S(1)}, f32[5,1,8,128]{3,2,1,0:T(8,128)S(1)}, u32[]{:S(2)}, u32[]{:S(2)}) %collective-permute-start.4) | collective-permute-done | bytes 20512 | tf_op jit(solution)/shard_map/ppermute | solution.py:24
  44.7 1.0 %collective-permute-start.6 = (f32[5,10,1,128]{3,2,1,0:T(1,128)S(1)}, f32[5,10,1,128]{3,2,1,0:T(1,128)S(1)}, u32[]{:S(2)}, u32[]{:S(2)}) collective-permute-start(f32[5,10,1,128]{3,2,1,0:T(1,128)S(1)} %get-tuple-element.138), channel_id=1, source_target_pairs={{0,1},{1,2},{2,3},{3,0},{4,5},{5,6},{6,7},{7,4},{8,9},{9,10},{10,1... | collective-permute-start | bytes 76808 | tf_op jit(solution)/shard_map/ppermute | solution.py:24
  45.7 2.9 %collective-permute-start.7 = (f32[5,10,1,128]{3,2,1,0:T(1,128)S(1)}, f32[5,10,1,128]{3,2,1,0:T(1,128)S(1)}, u32[]{:S(2)}, u32[]{:S(2)}) collective-permute-start(f32[5,10,1,128]{3,2,1,0:T(1,128)S(1)} %get-tuple-element.139), channel_id=1, source_target_pairs={{1,0},{2,1},{3,2},{0,3},{5,4},{6,5},{7,6},{4,7},{9,8},{10,9},{11,1... | collective-permute-start | bytes 76808 | tf_op jit(solution)/shard_map/ppermute | solution.py:27
  48.6 1.8 %collective-permute-done.6 = f32[5,10,1,128]{3,2,1,0:T(1,128)S(1)} collective-permute-done((f32[5,10,1,128]{3,2,1,0:T(1,128)S(1)}, f32[5,10,1,128]{3,2,1,0:T(1,128)S(1)}, u32[]{:S(2)}, u32[]{:S(2)}) %collective-permute-start.6) | collective-permute-done | bytes 25632 | tf_op jit(solution)/shard_map/ppermute | solution.py:24
  54.9 2.6 %collective-permute-start.9 = (f32[1,8,128]{2,1,0:T(8,128)S(1)}, f32[1,8,128]{2,1,0:T(8,128)S(1)}, u32[]{:S(2)}, u32[]{:S(2)}) collective-permute-start(f32[1,8,128]{2,1,0:T(8,128)S(1)} %get-tuple-element.277), channel_id=1, source_target_pairs={{4,0},{8,4},{12,8},{16,12},{20,16},{24,20},{28,24},{0,28},{5,1},{9... | collective-permute-start | bytes 12296 | tf_op jit(solution)/shard_map/ppermute | solution.py:27
  57.6 1.3 %collective-permute-done.8 = f32[1,8,128]{2,1,0:T(8,128)S(1)} collective-permute-done((f32[1,8,128]{2,1,0:T(8,128)S(1)}, f32[1,8,128]{2,1,0:T(8,128)S(1)}, u32[]{:S(2)}, u32[]{:S(2)}) %collective-permute-start.8) | collective-permute-done | bytes 4128 | tf_op jit(solution)/shard_map/ppermute | solution.py:24
  59.0 3.8 %collective-permute-start.11 = (f32[10,1,128]{2,1,0:T(1,128)S(1)}, f32[10,1,128]{2,1,0:T(1,128)S(1)}, u32[]{:S(2)}, u32[]{:S(2)}) collective-permute-start(f32[10,1,128]{2,1,0:T(1,128)S(1)} %get-tuple-element.271), channel_id=1, source_target_pairs={{1,0},{2,1},{3,2},{0,3},{5,4},{6,5},{7,6},{4,7},{9,8},{10,9},{11,1... | collective-permute-start | bytes 15368 | tf_op jit(solution)/shard_map/ppermute | solution.py:27
  62.9 1.5 %collective-permute-done.10 = f32[10,1,128]{2,1,0:T(1,128)S(1)} collective-permute-done((f32[10,1,128]{2,1,0:T(1,128)S(1)}, f32[10,1,128]{2,1,0:T(1,128)S(1)}, u32[]{:S(2)}, u32[]{:S(2)}) %collective-permute-start.10) | collective-permute-done | bytes 5152 | tf_op jit(solution)/shard_map/ppermute | solution.py:24
  66.1 0.8 copy-done.13
  67.1 2.6 %collective-permute-start.13 = (f32[1,8,128]{2,1,0:T(8,128)S(1)}, f32[1,8,128]{2,1,0:T(8,128)S(1)}, u32[]{:S(2)}, u32[]{:S(2)}) collective-permute-start(f32[1,8,128]{2,1,0:T(8,128)S(1)} %get-tuple-element.275), channel_id=1, source_target_pairs={{4,0},{8,4},{12,8},{16,12},{20,16},{24,20},{28,24},{0,28},{5,1},{9... | collective-permute-start | bytes 12296 | tf_op jit(solution)/shard_map/ppermute | solution.py:27
  69.7 1.3 %collective-permute-done.12 = f32[1,8,128]{2,1,0:T(8,128)S(1)} collective-permute-done((f32[1,8,128]{2,1,0:T(8,128)S(1)}, f32[1,8,128]{2,1,0:T(8,128)S(1)}, u32[]{:S(2)}, u32[]{:S(2)}) %collective-permute-start.12) | collective-permute-done | bytes 4128 | tf_op jit(solution)/shard_map/ppermute | solution.py:24
  71.1 1.2 %collective-permute-start.14 = (f32[10,1,128]{2,1,0:T(1,128)S(1)}, f32[10,1,128]{2,1,0:T(1,128)S(1)}, u32[]{:S(2)}, u32[]{:S(2)}) collective-permute-start(f32[10,1,128]{2,1,0:T(1,128)S(1)} %get-tuple-element.268), channel_id=1, source_target_pairs={{0,1},{1,2},{2,3},{3,0},{4,5},{5,6},{6,7},{7,4},{8,9},{9,10},{10,1... | collective-permute-start | bytes 15368 | tf_op jit(solution)/shard_map/ppermute | solution.py:24
  72.2 2.8 %collective-permute-start.15 = (f32[10,1,128]{2,1,0:T(1,128)S(1)}, f32[10,1,128]{2,1,0:T(1,128)S(1)}, u32[]{:S(2)}, u32[]{:S(2)}) collective-permute-start(f32[10,1,128]{2,1,0:T(1,128)S(1)} %get-tuple-element.269), channel_id=1, source_target_pairs={{1,0},{2,1},{3,2},{0,3},{5,4},{6,5},{7,6},{4,7},{9,8},{10,9},{11,1... | collective-permute-start | bytes 15368 | tf_op jit(solution)/shard_map/ppermute | solution.py:27
  75.1 1.5 %collective-permute-done.14 = f32[10,1,128]{2,1,0:T(1,128)S(1)} collective-permute-done((f32[10,1,128]{2,1,0:T(1,128)S(1)}, f32[10,1,128]{2,1,0:T(1,128)S(1)}, u32[]{:S(2)}, u32[]{:S(2)}) %collective-permute-start.14) | collective-permute-done | bytes 5152 | tf_op jit(solution)/shard_map/ppermute | solution.py:24
  78.3 0.8 copy-done.15
  79.3 2.6 %collective-permute-start.17 = (f32[1,8,128]{2,1,0:T(8,128)S(1)}, f32[1,8,128]{2,1,0:T(8,128)S(1)}, u32[]{:S(2)}, u32[]{:S(2)}) collective-permute-start(f32[1,8,128]{2,1,0:T(8,128)S(1)} %get-tuple-element.273), channel_id=1, source_target_pairs={{4,0},{8,4},{12,8},{16,12},{20,16},{24,20},{28,24},{0,28},{5,1},{9... | collective-permute-start | bytes 12296 | tf_op jit(solution)/shard_map/ppermute | solution.py:27
  83.3 1.3 %collective-permute-start.18 = (f32[10,1,128]{2,1,0:T(1,128)S(1)}, f32[10,1,128]{2,1,0:T(1,128)S(1)}, u32[]{:S(2)}, u32[]{:S(2)}) collective-permute-start(f32[10,1,128]{2,1,0:T(1,128)S(1)} %get-tuple-element.266), channel_id=1, source_target_pairs={{0,1},{1,2},{2,3},{3,0},{4,5},{5,6},{6,7},{7,4},{8,9},{9,10},{10,1... | collective-permute-start | bytes 15368 | tf_op jit(solution)/shard_map/ppermute | solution.py:24
  84.6 2.7 %collective-permute-start.19 = (f32[10,1,128]{2,1,0:T(1,128)S(1)}, f32[10,1,128]{2,1,0:T(1,128)S(1)}, u32[]{:S(2)}, u32[]{:S(2)}) collective-permute-start(f32[10,1,128]{2,1,0:T(1,128)S(1)} %get-tuple-element.267), channel_id=1, source_target_pairs={{1,0},{2,1},{3,2},{0,3},{5,4},{6,5},{7,6},{4,7},{9,8},{10,9},{11,1... | collective-permute-start | bytes 15368 | tf_op jit(solution)/shard_map/ppermute | solution.py:27
  87.9 0.9 collective-permute-done.18
  90.5 0.8 copy-done.11
  (346 shorter events, 24.9 us)
Async XLA Ops:
  0.6 6.7 %copy-start.8 = (f32[3,8,8,128]{3,2,1,0:T(8,128)S(1)}, f32[3,8,8,128]{3,2,1,0:T(8,128)}, u32[]{:S(2)}) copy-start(f32[3,8,8,128]{3,2,1,0:T(8,128)} %param.7) | copy-start | bytes 294916
  0.6 6.7 %copy-start.9 = (f32[3,8,8,128]{3,2,1,0:T(8,128)S(1)}, f32[3,8,8,128]{3,2,1,0:T(8,128)}, u32[]{:S(2)}) copy-start(f32[3,8,8,128]{3,2,1,0:T(8,128)} %param.5) | copy-start | bytes 294916
  0.7 6.7 %copy-start.16 = (f32[8,8,128]{2,1,0:T(8,128)S(1)}, f32[8,8,128]{2,1,0:T(8,128)}, u32[]{:S(2)}) copy-start(f32[8,8,128]{2,1,0:T(8,128)} %param.6) | copy-start | bytes 98308
  0.7 6.7 %copy-start.17 = (f32[8,8,128]{2,1,0:T(8,128)S(1)}, f32[8,8,128]{2,1,0:T(8,128)}, u32[]{:S(2)}) copy-start(f32[8,8,128]{2,1,0:T(8,128)} %param.4) | copy-start | bytes 98308
  1.6 5.7 %collective-permute-start = (f32[8,3,8,128]{3,2,1,0:T(8,128)S(1)}, f32[8,3,8,128]{3,2,1,0:T(8,128)S(1)}, u32[]{:S(2)}, u32[]{:S(2)}) collective-permute-start(f32[8,3,8,128]{3,2,1,0:T(8,128)S(1)} %get-tuple-element.136), channel_id=1, source_target_pairs={{0,4},{4,8},{8,12},{12,16},{16,20},{20,24},{24,28},{28,0},{1,5},{5... | collective-permute-start | bytes 294920 | tf_op jit(solution)/shard_map/ppermute | solution.py:24
  2.1 5.2 %collective-permute-start.1 = (f32[8,3,8,128]{3,2,1,0:T(8,128)S(1)}, f32[8,3,8,128]{3,2,1,0:T(8,128)S(1)}, u32[]{:S(2)}, u32[]{:S(2)}) collective-permute-start(f32[8,3,8,128]{3,2,1,0:T(8,128)S(1)} %get-tuple-element.137), channel_id=1, source_target_pairs={{4,0},{8,4},{12,8},{16,12},{20,16},{24,20},{28,24},{0,28},{5,1},{9... | collective-permute-start | bytes 294920 | tf_op jit(solution)/shard_map/ppermute | solution.py:27
  7.5 10.8 %collective-permute-start.2 = (f32[8,14,3,128]{3,2,1,0:T(4,128)S(1)}, f32[8,14,3,128]{3,2,1,0:T(4,128)S(1)}, u32[]{:S(2)}, u32[]{:S(2)}) collective-permute-start(f32[8,14,3,128]{3,2,1,0:T(4,128)S(1)} %get-tuple-element.125), channel_id=1, source_target_pairs={{0,1},{1,2},{2,3},{3,0},{4,5},{5,6},{6,7},{7,4},{8,9},{9,10},{10,1... | collective-permute-start | bytes 516104 | tf_op jit(solution)/shard_map/ppermute | solution.py:24
  9.8 13.1 %collective-permute-start.3 = (f32[8,14,3,128]{3,2,1,0:T(4,128)S(1)}, f32[8,14,3,128]{3,2,1,0:T(4,128)S(1)}, u32[]{:S(2)}, u32[]{:S(2)}) collective-permute-start(f32[8,14,3,128]{3,2,1,0:T(4,128)S(1)} %get-tuple-element.126), channel_id=1, source_target_pairs={{1,0},{2,1},{3,2},{0,3},{5,4},{6,5},{7,6},{4,7},{9,8},{10,9},{11,1... | collective-permute-start | bytes 516104 | tf_op jit(solution)/shard_map/ppermute | solution.py:27
  36.3 1.0 %slice-start.4 = ((f32[14,14,128]{2,1,0:T(8,128)}), f32[13,14,128]{2,1,0:T(8,128)S(1)}, s32[]{:S(2)}) async-start(f32[14,14,128]{2,1,0:T(8,128)} %copy-done.4), calls=%async_computation.4 | async-start | bytes 212992 | tf_op jit(solution)/shard_map/jit(_roll_static)/slice | solution.py:33
  38.0 1.0 %slice-start.6 = ((f32[14,14,128]{2,1,0:T(8,128)}), f32[13,14,128]{2,1,0:T(8,128)S(1)}, s32[]{:S(2)}) async-start(f32[14,14,128]{2,1,0:T(8,128)} %copy-done.6), calls=%async_computation.6 | async-start | bytes 212992 | tf_op jit(solution)/shard_map/jit(_roll_static)/slice | solution.py:33
  40.5 4.2 %collective-permute-start.4 = (f32[5,1,8,128]{3,2,1,0:T(8,128)S(1)}, f32[5,1,8,128]{3,2,1,0:T(8,128)S(1)}, u32[]{:S(2)}, u32[]{:S(2)}) collective-permute-start(f32[5,1,8,128]{3,2,1,0:T(8,128)S(1)} %get-tuple-element.146), channel_id=1, source_target_pairs={{0,4},{4,8},{8,12},{12,16},{16,20},{20,24},{24,28},{28,0},{1,5},{5... | collective-permute-start | bytes 61448 | tf_op jit(solution)/shard_map/ppermute | solution.py:24
  40.6 4.1 %collective-permute-start.5 = (f32[5,1,8,128]{3,2,1,0:T(8,128)S(1)}, f32[5,1,8,128]{3,2,1,0:T(8,128)S(1)}, u32[]{:S(2)}, u32[]{:S(2)}) collective-permute-start(f32[5,1,8,128]{3,2,1,0:T(8,128)S(1)} %get-tuple-element.147), channel_id=1, source_target_pairs={{4,0},{8,4},{12,8},{16,12},{20,16},{24,20},{28,24},{0,28},{5,1},{9... | collective-permute-start | bytes 61448 | tf_op jit(solution)/shard_map/ppermute | solution.py:27
  44.7 5.7 %collective-permute-start.6 = (f32[5,10,1,128]{3,2,1,0:T(1,128)S(1)}, f32[5,10,1,128]{3,2,1,0:T(1,128)S(1)}, u32[]{:S(2)}, u32[]{:S(2)}) collective-permute-start(f32[5,10,1,128]{3,2,1,0:T(1,128)S(1)} %get-tuple-element.138), channel_id=1, source_target_pairs={{0,1},{1,2},{2,3},{3,0},{4,5},{5,6},{6,7},{7,4},{8,9},{9,10},{10,1... | collective-permute-start | bytes 76808 | tf_op jit(solution)/shard_map/ppermute | solution.py:24
  45.7 4.7 %collective-permute-start.7 = (f32[5,10,1,128]{3,2,1,0:T(1,128)S(1)}, f32[5,10,1,128]{3,2,1,0:T(1,128)S(1)}, u32[]{:S(2)}, u32[]{:S(2)}) collective-permute-start(f32[5,10,1,128]{3,2,1,0:T(1,128)S(1)} %get-tuple-element.139), channel_id=1, source_target_pairs={{1,0},{2,1},{3,2},{0,3},{5,4},{6,5},{7,6},{4,7},{9,8},{10,9},{11,1... | collective-permute-start | bytes 76808 | tf_op jit(solution)/shard_map/ppermute | solution.py:27
  53.2 1.0 %slice-start.1 = ((f32[10,10,128]{2,1,0:T(8,128)}), f32[9,10,128]{2,1,0:T(8,128)S(1)}, s32[]{:S(2)}) async-start(f32[10,10,128]{2,1,0:T(8,128)} %copy-done), calls=%async_computation.1 | async-start | bytes 147456 | tf_op jit(solution)/shard_map/jit(_roll_static)/slice | solution.py:33
  53.2 1.0 %copy-start.3 = (f32[10,10,128]{2,1,0:T(8,128)S(1)}, f32[10,10,128]{2,1,0:T(8,128)}, u32[]{:S(2)}) copy-start(f32[10,10,128]{2,1,0:T(8,128)} %copy-done.2) | copy-start | bytes 153604
  53.2 1.0 %slice-start.2 = ((f32[10,10,128]{2,1,0:T(8,128)}), f32[9,10,128]{2,1,0:T(8,128)S(1)}, s32[]{:S(2)}) async-start(f32[10,10,128]{2,1,0:T(8,128)} %copy-done.2), calls=%async_computation.2 | async-start | bytes 147456 | tf_op jit(solution)/shard_map/jit(_roll_static)/slice | solution.py:33
  54.9 4.0 %collective-permute-start.8 = (f32[1,8,128]{2,1,0:T(8,128)S(1)}, f32[1,8,128]{2,1,0:T(8,128)S(1)}, u32[]{:S(2)}, u32[]{:S(2)}) collective-permute-start(f32[1,8,128]{2,1,0:T(8,128)S(1)} %get-tuple-element.276), channel_id=1, source_target_pairs={{0,4},{4,8},{8,12},{12,16},{16,20},{20,24},{24,28},{28,0},{1,5},{5... | collective-permute-start | bytes 12296 | tf_op jit(solution)/shard_map/ppermute | solution.py:24
  54.9 4.0 %collective-permute-start.9 = (f32[1,8,128]{2,1,0:T(8,128)S(1)}, f32[1,8,128]{2,1,0:T(8,128)S(1)}, u32[]{:S(2)}, u32[]{:S(2)}) collective-permute-start(f32[1,8,128]{2,1,0:T(8,128)S(1)} %get-tuple-element.277), channel_id=1, source_target_pairs={{4,0},{8,4},{12,8},{16,12},{20,16},{24,20},{28,24},{0,28},{5,1},{9... | collective-permute-start | bytes 12296 | tf_op jit(solution)/shard_map/ppermute | solution.py:27
  58.9 5.5 %collective-permute-start.10 = (f32[10,1,128]{2,1,0:T(1,128)S(1)}, f32[10,1,128]{2,1,0:T(1,128)S(1)}, u32[]{:S(2)}, u32[]{:S(2)}) collective-permute-start(f32[10,1,128]{2,1,0:T(1,128)S(1)} %get-tuple-element.270), channel_id=1, source_target_pairs={{0,1},{1,2},{2,3},{3,0},{4,5},{5,6},{6,7},{7,4},{8,9},{9,10},{10,1... | collective-permute-start | bytes 15368 | tf_op jit(solution)/shard_map/ppermute | solution.py:24
  59.0 5.4 %collective-permute-start.11 = (f32[10,1,128]{2,1,0:T(1,128)S(1)}, f32[10,1,128]{2,1,0:T(1,128)S(1)}, u32[]{:S(2)}, u32[]{:S(2)}) collective-permute-start(f32[10,1,128]{2,1,0:T(1,128)S(1)} %get-tuple-element.271), channel_id=1, source_target_pairs={{1,0},{2,1},{3,2},{0,3},{5,4},{6,5},{7,6},{4,7},{9,8},{10,9},{11,1... | collective-permute-start | bytes 15368 | tf_op jit(solution)/shard_map/ppermute | solution.py:27
  66.0 1.0 %slice-start.8 = ((f32[10,10,128]{2,1,0:T(8,128)}), f32[9,10,128]{2,1,0:T(8,128)S(1)}, s32[]{:S(2)}) async-start(f32[10,10,128]{2,1,0:T(8,128)} %copy-done.12), calls=%async_computation.8 | async-start | bytes 147456 | tf_op jit(solution)/shard_map/jit(_roll_static)/slice | solution.py:33
  67.0 4.0 %collective-permute-start.12 = (f32[1,8,128]{2,1,0:T(8,128)S(1)}, f32[1,8,128]{2,1,0:T(8,128)S(1)}, u32[]{:S(2)}, u32[]{:S(2)}) collective-permute-start(f32[1,8,128]{2,1,0:T(8,128)S(1)} %get-tuple-element.274), channel_id=1, source_target_pairs={{0,4},{4,8},{8,12},{12,16},{16,20},{20,24},{24,28},{28,0},{1,5},{5... | collective-permute-start | bytes 12296 | tf_op jit(solution)/shard_map/ppermute | solution.py:24
  67.1 4.0 %collective-permute-start.13 = (f32[1,8,128]{2,1,0:T(8,128)S(1)}, f32[1,8,128]{2,1,0:T(8,128)S(1)}, u32[]{:S(2)}, u32[]{:S(2)}) collective-permute-start(f32[1,8,128]{2,1,0:T(8,128)S(1)} %get-tuple-element.275), channel_id=1, source_target_pairs={{4,0},{8,4},{12,8},{16,12},{20,16},{24,20},{28,24},{0,28},{5,1},{9... | collective-permute-start | bytes 12296 | tf_op jit(solution)/shard_map/ppermute | solution.py:27
  71.1 5.5 %collective-permute-start.14 = (f32[10,1,128]{2,1,0:T(1,128)S(1)}, f32[10,1,128]{2,1,0:T(1,128)S(1)}, u32[]{:S(2)}, u32[]{:S(2)}) collective-permute-start(f32[10,1,128]{2,1,0:T(1,128)S(1)} %get-tuple-element.268), channel_id=1, source_target_pairs={{0,1},{1,2},{2,3},{3,0},{4,5},{5,6},{6,7},{7,4},{8,9},{9,10},{10,1... | collective-permute-start | bytes 15368 | tf_op jit(solution)/shard_map/ppermute | solution.py:24
  72.2 4.4 %collective-permute-start.15 = (f32[10,1,128]{2,1,0:T(1,128)S(1)}, f32[10,1,128]{2,1,0:T(1,128)S(1)}, u32[]{:S(2)}, u32[]{:S(2)}) collective-permute-start(f32[10,1,128]{2,1,0:T(1,128)S(1)} %get-tuple-element.269), channel_id=1, source_target_pairs={{1,0},{2,1},{3,2},{0,3},{5,4},{6,5},{7,6},{4,7},{9,8},{10,9},{11,1... | collective-permute-start | bytes 15368 | tf_op jit(solution)/shard_map/ppermute | solution.py:27
  78.2 1.0 %slice-start.9 = ((f32[10,10,128]{2,1,0:T(8,128)}), f32[9,10,128]{2,1,0:T(8,128)S(1)}, s32[]{:S(2)}) async-start(f32[10,10,128]{2,1,0:T(8,128)} %copy-done.14), calls=%async_computation.9 | async-start | bytes 147456 | tf_op jit(solution)/shard_map/jit(_roll_static)/slice | solution.py:33
  79.2 4.0 %collective-permute-start.16 = (f32[1,8,128]{2,1,0:T(8,128)S(1)}, f32[1,8,128]{2,1,0:T(8,128)S(1)}, u32[]{:S(2)}, u32[]{:S(2)}) collective-permute-start(f32[1,8,128]{2,1,0:T(8,128)S(1)} %get-tuple-element.272), channel_id=1, source_target_pairs={{0,4},{4,8},{8,12},{12,16},{16,20},{20,24},{24,28},{28,0},{1,5},{5... | collective-permute-start | bytes 12296 | tf_op jit(solution)/shard_map/ppermute | solution.py:24
  79.3 4.0 %collective-permute-start.17 = (f32[1,8,128]{2,1,0:T(8,128)S(1)}, f32[1,8,128]{2,1,0:T(8,128)S(1)}, u32[]{:S(2)}, u32[]{:S(2)}) collective-permute-start(f32[1,8,128]{2,1,0:T(8,128)S(1)} %get-tuple-element.273), channel_id=1, source_target_pairs={{4,0},{8,4},{12,8},{16,12},{20,16},{24,20},{28,24},{0,28},{5,1},{9... | collective-permute-start | bytes 12296 | tf_op jit(solution)/shard_map/ppermute | solution.py:27
  83.3 5.5 %collective-permute-start.18 = (f32[10,1,128]{2,1,0:T(1,128)S(1)}, f32[10,1,128]{2,1,0:T(1,128)S(1)}, u32[]{:S(2)}, u32[]{:S(2)}) collective-permute-start(f32[10,1,128]{2,1,0:T(1,128)S(1)} %get-tuple-element.266), channel_id=1, source_target_pairs={{0,1},{1,2},{2,3},{3,0},{4,5},{5,6},{6,7},{7,4},{8,9},{9,10},{10,1... | collective-permute-start | bytes 15368 | tf_op jit(solution)/shard_map/ppermute | solution.py:24
  84.6 4.2 %collective-permute-start.19 = (f32[10,1,128]{2,1,0:T(1,128)S(1)}, f32[10,1,128]{2,1,0:T(1,128)S(1)}, u32[]{:S(2)}, u32[]{:S(2)}) collective-permute-start(f32[10,1,128]{2,1,0:T(1,128)S(1)} %get-tuple-element.267), channel_id=1, source_target_pairs={{1,0},{2,1},{3,2},{0,3},{5,4},{6,5},{7,6},{4,7},{9,8},{10,9},{11,1... | collective-permute-start | bytes 15368 | tf_op jit(solution)/shard_map/ppermute | solution.py:27
  90.4 1.0 %slice-start.7 = ((f32[10,10,128]{2,1,0:T(8,128)}), f32[9,10,128]{2,1,0:T(8,128)S(1)}, s32[]{:S(2)}) async-start(f32[10,10,128]{2,1,0:T(8,128)} %copy-done.10), calls=%async_computation.7 | async-start | bytes 147456 | tf_op jit(solution)/shard_map/jit(_roll_static)/slice | solution.py:33
  (16 other events, 12.5 us)
where the time goes:
time: 92.4 us; the launch traced here: 92 us
  starting transfers between devices  34.5 us (37%)
  waiting for transfers between devices  23.8 us (26%)
  local copies, waits for them, and re-layouts  16 us (17%)
  other arithmetic  15 us (16%)
  between operations  2.72 us (3%)
    ppermute x10, starting transfers between devices, extended_2(): lax.ppermute(lax.slice_in_dim(block, 0, width, axis=dim), axis, backward)  27.8 us
    ppermute x10, waiting for transfers between devices, extended_2(): lax.ppermute(lax.slice_in_dim(block, block.shape[dim] - width, None, axis...  18.9 us
    unnamed x39, local copies, waits for them, and re-layouts  9.62 us
    ppermute x10, starting transfers between devices, extended_2(): lax.ppermute(lax.slice_in_dim(block, block.shape[dim] - width, None, axis...  6.67 us
    sub x17, other arithmetic, face_fluxes(): 0.5 * (flux_lower[n] + flux_upper[n])  6.48 us
    slice x207, local copies, waits for them, and re-layouts, adjacent_zone(): return jnp.roll(a, -k, dimension)  6.22 us
    ppermute x10, waiting for transfers between devices, extended_2(): lax.ppermute(lax.slice_in_dim(block, 0, width, axis=dim), axis, backward)  4.82 us
  transfers between devices with their start and end apart: 20, of which 11 were waited for; matrix products, arithmetic and copies ran while one was open for 1% of the time, Pallas kernels for 0%

commit v1 on v0

v1 whole, which is shorter than its diff:
```python
import functools

import jax
import jax.numpy as jnp
from jax import lax
from jax.experimental import pallas as pl
from jax.experimental.pallas import tpu as pltpu
from jax.sharding import PartitionSpec as P

SECTIONS = 4
SUPER_SECTIONS = 8

G = 5.0 / 3.0
DT = 0.04
SUPER_TIME = 0.08
DENSITY_FLOOR = 0.5
PRESSURE_FLOOR = 0.1
FIELD_FLOOR = 0.05

MESH = pl.DeviceIdType.MESH

H = 3
ROWS = 16


def ylow(a):
    return pltpu.roll(a, 1, 0)


def yhigh(a):
    return pltpu.roll(a, a.shape[0] - 1, 0)


def zlow(a):
    return pltpu.roll(a, 1, 1)


def zhigh(a):
    return pltpu.roll(a, a.shape[1] - 1, 1)


def minmod(a, b):
    return jnp.maximum(jnp.minimum(a, b), 0.0) + jnp.minimum(jnp.maximum(a, b), 0.0)


def wave(rho, v, p, b, d):
    bsq = b[0] * b[0] + b[1] * b[1] + b[2] * b[2]
    ksq = v[0] * v[0] + v[1] * v[1] + v[2] * v[2]
    half = 0.5 * bsq
    energy = p * 1.5 + 0.5 * rho * ksq + half
    total = p + half
    vn, bn = v[d], b[d]
    proj = v[0] * b[0] + v[1] * b[1] + v[2] * b[2]
    others = [c for c in range(3) if c != d]
    m = [rho * v[c] for c in range(3)]
    cons = [rho] + m + [energy] + [b[c] for c in others]
    mom = []
    for c in range(3):
        t = m[d] * v[c] - bn * b[c]
        mom.append(t + total if c == d else t)
    flux = [m[d]] + mom + [(energy + total) * vn - bn * proj]
    flux += [vn * b[c] - v[c] * bn for c in others]
    a = G * p + bsq
    signal = jnp.abs(vn) + a * lax.rsqrt(a * rho)
    return cons, flux, signal


def face_flux(lower, upper, bn, d):
    def split(s):
        rest = list(s[5:])
        rest.insert(d, bn)
        return s[0], s[1:4], s[4], rest

    ul, fl, sl = wave(*split(lower), d)
    uu, fu, su = wave(*split(upper), d)
    signal = jnp.maximum(sl, su)
    return [0.5 * ((fl[n] + fu[n]) - signal * (uu[n] - ul[n])) for n in range(7)]


def along(prims, bn, d):
    low, high = (ylow, yhigh) if d == 1 else (zlow, zhigh)
    lower, upper = [], []
    for q in prims:
        diff = q - low(q)
        half = 0.5 * minmod(diff, high(diff))
        lower.append(low(q + half))
        upper.append(q - half)
    return face_flux(lower, upper, bn, d)


def rkl_factors():
    b = [1.0 / 3.0] * 3 + [
        (j * j + j - 2.0) / (2.0 * j * (j + 1.0)) for j in range(3, SUPER_SECTIONS + 1)
    ]
    w = 4.0 / (SUPER_SECTIONS * SUPER_SECTIONS + SUPER_SECTIONS - 2.0)
    rows = []
    for j in range(2, SECTIONS + 1):
        mu = (2.0 * j - 1.0) / j * b[j] / b[j - 1]
        nu = -(j - 1.0) / j * b[j] / b[j - 2]
        rate = mu * w * SUPER_TIME
        rows.append((mu, nu, 1.0 - mu - nu, rate, -(1.0 - b[j - 1]) * rate))
    return b[1] * w * SUPER_TIME, rows


def kernel(
    nx, ny,
    rho_ref, v_ref, p_ref, b_ref,
    o_rho, o_v, o_p, o_b,
    ext, up, down, from_low, from_high,
    lower_s, diff_s, cell_s, d_s, f_s, b_s,
    irho_s, e_s, kap_s, bc_s, bf_s, kx_s, ky_s, kz_s,
    t_s, pk, low_row, high_row,
    send_sem, recv_sem,
):
    cx = rho_ref.shape[0]
    cy = rho_ref.shape[1]
    gx, gy = lax.axis_index("gx"), lax.axis_index("gy")

    def target(dx, dy):
        return (lax.rem(gx + dx + nx, nx), lax.rem(gy + dy + ny, ny))

    ring = [(dx, dy) for dy in (1, -1, 0) for dx in (0, 1, -1) if (dx, dy) != (0, 0)]

    barrier = pltpu.get_barrier_semaphore()
    for dx, dy in ring:
        pl.semaphore_signal(barrier, inc=1, device_id=target(dx, dy), device_id_type=MESH)

    fields = [rho_ref] + [v_ref.at[c] for c in range(3)] + [p_ref] + [b_ref.at[c] for c in range(3)]
    for f, ref in enumerate(fields):
        value = ref[...]
        up[:, H * f : H * f + H, :] = value[:, cy - H : cy, :]
        down[:, H * f : H * f + H, :] = value[:, 0:H, :]
        ext[f, H : H + cx, 0:cy, :] = value
    pl.semaphore_wait(barrier, len(ring))

    def remote(phase, k, src, dst):
        copy = pltpu.make_async_remote_copy(
            src_ref=src,
            dst_ref=dst,
            send_sem=send_sem.at[phase, k],
            recv_sem=recv_sem.at[phase, k],
            device_id=target(*ring[k]),
            device_id_type=MESH,
        )
        copy.start()
        return copy

    copies = []
    for k, (dx, dy) in enumerate(ring):
        if dx == 0:
            here, there = slice(0, cx), slice(H, H + cx)
        elif dx == 1:
            here, there = slice(cx - H, cx), slice(0, H)
        else:
            here, there = slice(0, H), slice(H + cx, 2 * H + cx)
        here = pl.ds(here.start, here.stop - here.start)
        there = pl.ds(there.start, there.stop - there.start)
        if dy == 1:
            copies.append(remote(0, k, up.at[here], from_low.at[there]))
        elif dy == -1:
            copies.append(remote(0, k, down.at[here], from_high.at[there]))
        else:
            src = pl.ds(here.start + H, here.size)
            copies.append(
                remote(0, k, ext.at[:, src, pl.ds(0, cy)], ext.at[:, there, pl.ds(0, cy)])
            )

    one = jnp.ones((ROWS, 128), jnp.float32)
    for ref in (lower_s, diff_s, cell_s, d_s, f_s, b_s):
        for n in range(ref.shape[0]):
            ref[n] = one
    for copy in copies:
        copy.wait()

    def unpack(s, carry):
        for f in range(8):
            ext[f, s, cy:ROWS, :] = jnp.ones((ROWS - cy, 128), jnp.float32)
            ext[f, s, cy : cy + H, :] = from_high[s, H * f : H * f + H, :]
            ext[f, s, ROWS - H : ROWS, :] = from_low[s, H * f : H * f + H, :]
        return carry

    lax.fori_loop(0, cx + 2 * H, unpack, 0)

    def cells(s):
        by, bz = ext[6, s], ext[7, s]
        return [0.5 * (by + yhigh(by)), 0.5 * (bz + zhigh(bz))]

    def raw(s):
        return [ext[f, s] for f in range(5)] + cells(s)

    first, second = raw(0), raw(1)
    for n in range(7):
        diff_s[n] = second[n] - first[n]
    cell_s[0] = second[5]
    cell_s[1] = second[6]

    def body(i, carry):
        here = [ext[f, i] for f in range(5)] + [cell_s[0], cell_s[1]]
        there = raw(i + 1)
        bx, by, bz = ext[5, i], ext[6, i], ext[7, i]
        cell = [0.5 * (bx + ext[5, i + 1]), here[5], here[6]]
        lower = [lower_s[n] for n in range(7)]
        upper = []
        for n in range(7):
            diff = there[n] - here[n]
            half = 0.5 * minmod(diff_s[n], diff)
            diff_s[n] = diff
            upper.append(here[n] - half)
            lower_s[n] = here[n] + half
        cell_s[0] = there[5]
        cell_s[1] = there[6]
        fx = face_flux(lower, upper, bx, 0)
        fy = along(here[:5] + [cell[0], cell[2]], by, 1)
        fz = along(here[:5] + [cell[0], cell[1]], bz, 2)

        ez = 0.25 * (f_s[0] + fy[5] - ylow(fx[5]) - fx[5])
        ey = 0.25 * (zlow(fx[6]) + fx[6] - f_s[1] - fz[5])
        ex = 0.25 * (ylow(fz[6]) + fz[6] - zlow(fy[6]) - fy[6])
        f_s[0] = fy[5]
        f_s[1] = fz[5]
        bxn = bx - DT * (yhigh(ez) - ez) + DT * (zhigh(ey) - ey)
        bxo = b_s[0]
        byn = b_s[1] + DT * ez
        bzn = b_s[2] - DT * ey
        b_s[0] = bxn
        b_s[1] = by - DT * (zhigh(ex) - ex) - DT * ez
        b_s[2] = bz + DT * ey + DT * (yhigh(ex) - ex)

        rho, v, p = here[0], here[1:4], here[4]
        energy = (
            p * 1.5
            + 0.5 * rho * (v[0] * v[0] + v[1] * v[1] + v[2] * v[2])
            + 0.5 * (cell[0] * cell[0] + cell[1] * cell[1] + cell[2] * cell[2])
        )
        cons = [rho, rho * v[0], rho * v[1], rho * v[2], energy]
        new = [d_s[n] - DT * fx[n] for n in range(5)]
        for n in range(5):
            d_s[n] = cons[n] - DT * ((yhigh(fy[n]) - fy[n]) + (zhigh(fz[n]) - fz[n]) - fx[n])

        m = i - 1
        floored = jnp.maximum(new[0], DENSITY_FLOOR)
        inv = 1.0 / floored
        vel = [new[1 + c] * inv for c in range(3)]
        bc = [0.5 * (bxo + bxn), 0.5 * (byn + yhigh(byn)), 0.5 * (bzn + zhigh(bzn))]
        kinetic = new[1] * vel[0] + new[2] * vel[1] + new[3] * vel[2]
        internal = new[4] - 0.5 * kinetic - 0.5 * (bc[0] * bc[0] + bc[1] * bc[1] + bc[2] * bc[2])
        p1 = jnp.maximum((G - 1.0) * internal, PRESSURE_FLOOR)
        t = p1 * inv
        irho_s[m] = (G - 1.0) * inv
        e_s[m] = p1 * 1.5
        t_s[0, m] = t
        kap_s[m] = t * t * jnp.sqrt(t)
        for c in range(3):
            bc_s[c, m] = bc[c]
        for c, a in enumerate((bxo, byn, bzn)):
            bf_s[c, m] = a

        @pl.when(jnp.logical_and(m >= H, m < H + cx))
        def _():
            x = jnp.clip(m - H, 0, cx - 1)
            o_rho[x] = floored[0:cy]
            for c in range(3):
                o_v[c, x] = vel[c][0:cy]
            for c, a in enumerate((bxo, byn, bzn)):
                o_b[c, x] = a[0:cy]

        return carry

    lax.fori_loop(1, cx + 2 * H - 1, body, 0)

    def coupling(s, carry):
        kap = kap_s[s]
        bc = [bc_s[c, s] for c in range(3)]
        bf = [bf_s[c, s] for c in range(3)]
        for d, out in enumerate((kx_s, ky_s, kz_s)):
            if d == 0:
                kl, bl = kap_s[s - 1], [bc_s[c, s - 1] for c in range(3)]
            else:
                low = ylow if d == 1 else zlow
                kl, bl = low(kap), [low(bc[c]) if c != d else None for c in range(3)]
            comp = [bf[d] if c == d else 0.5 * (bc[c] + bl[c]) for c in range(3)]
            mag = comp[0] * comp[0] + comp[1] * comp[1] + comp[2] * comp[2]
            factor = 0.5 * (kap + kl) / jnp.maximum(mag, FIELD_FLOOR) * bf[d]
            rows = ROWS if d == 1 else cy
            for c in range(3):
                k = factor * comp[c] * (1.0 if c == d else 0.25)
                out[c, s - H] = k[0:rows]
        return carry

    lax.fori_loop(H, H + cx + 1, coupling, 0)

    def rate(phase):
        t = [t_s[phase, H - 1 + s] for s in range(cx + 2)]
        ts = [a[0:cy] for a in t]
        dz = [zhigh(a) - zlow(a) for a in t]
        dy = [(yhigh(a) - ylow(a))[0:cy] for a in t]
        out = []
        qx = []
        for x in range(cx + 1):
            qx.append(
                kx_s[0, x] * (ts[x + 1] - ts[x])
                + kx_s[1, x] * (dy[x] + dy[x + 1])
                + kx_s[2, x] * (dz[x] + dz[x + 1])[0:cy]
            )
        for x in range(cx):
            a = t[x + 1]
            dx = t[x + 2] - t[x]
            qy = (
                ky_s[1, x] * (a - ylow(a))
                + ky_s[0, x] * (dx + ylow(dx))
                + ky_s[2, x] * (dz[x + 1] + ylow(dz[x + 1]))
            )
            dxs = dx[0:cy]
            qz = (
                kz_s[2, x] * (ts[x + 1] - zlow(ts[x + 1]))
                + kz_s[0, x] * (dxs + zlow(dxs))
                + kz_s[1, x] * (dy[x + 1] + zlow(dy[x + 1]))
            )
            out.append(qx[x + 1] - qx[x] + (yhigh(qy) - qy)[0:cy] + (zhigh(qz) - qz))
        return jnp.stack(out)

    first_factor, factors = rkl_factors()
    inner = pl.ds(H, cx)
    base = e_s[inner, 0:cy, :]
    irho = irho_s[inner, 0:cy, :]
    rate0 = rate(0)
    earlier, latest = base, base + first_factor * rate0
    for n, (mu, nu, rest, fresh, zero) in enumerate(factors):
        phase = n + 1
        t = latest * irho
        for x in range(cx):
            pk[n, 0, x : x + 1, :] = t[x, cy - 1 : cy, :]
            pk[n, 1, x : x + 1, :] = t[x, 0:1, :]
        t_s[phase, inner, 0:cy, :] = t
        copies = []
        for k, (dx, dy) in enumerate(ring):
            if dy == 1:
                copies.append(remote(phase, k, pk.at[n, 0], low_row.at[n, dx + 1]))
            elif dy == -1:
                copies.append(remote(phase, k, pk.at[n, 1], high_row.at[n, dx + 1]))
            else:
                src = H + cx - 1 if dx == 1 else H
                dst = H - 1 if dx == 1 else H + cx
                copies.append(
                    remote(
                        phase, k,
                        t_s.at[phase, src, pl.ds(0, cy)],
                        t_s.at[phase, dst, pl.ds(0, cy)],
                    )
                )
        part = mu * latest + nu * earlier + rest * base + zero * rate0
        for copy in copies:
            copy.wait()
        for s in range(cx + 2):
            if s == 0:
                d, x = 2, cx - 1
            elif s == cx + 1:
                d, x = 0, 0
            else:
                d, x = 1, s - 1
            t_s[phase, H - 1 + s, cy : cy + 1, :] = high_row[n, d, x : x + 1, :]
            t_s[phase, H - 1 + s, ROWS - 1 : ROWS, :] = low_row[n, d, x : x + 1, :]
        earlier, latest = latest, part + fresh * rate(phase)
    o_p[...] = (G - 1.0) * latest


def solution(mesh):
    nx, ny = mesh.shape["gx"], mesh.shape["gy"]

    def local(rho, v, p, b):
        cx, cy, nz = rho.shape
        wide = cx + 2 * H
        f32 = jnp.float32
        vm = lambda *shape: pltpu.VMEM(shape, f32)
        phases = SECTIONS - 1
        spec = pl.BlockSpec(memory_space=pltpu.VMEM)
        return pl.pallas_call(
            functools.partial(kernel, nx, ny),
            out_shape=[
                jax.ShapeDtypeStruct(rho.shape, f32),
                jax.ShapeDtypeStruct(v.shape, f32),
                jax.ShapeDtypeStruct(p.shape, f32),
                jax.ShapeDtypeStruct(b.shape, f32),
            ],
            in_specs=[spec] * 4,
            out_specs=[spec] * 4,
            scratch_shapes=[
                vm(8, wide, ROWS, nz),
                vm(cx, 8 * H, nz),
                vm(cx, 8 * H, nz),
                vm(wide, 8 * H, nz),
                vm(wide, 8 * H, nz),
                vm(7, ROWS, nz),
                vm(7, ROWS, nz),
                vm(2, ROWS, nz),
                vm(5, ROWS, nz),
                vm(2, ROWS, nz),
                vm(3, ROWS, nz),
                vm(wide, ROWS, nz),
                vm(wide, ROWS, nz),
                vm(wide, ROWS, nz),
                vm(3, wide, ROWS, nz),
                vm(3, wide, ROWS, nz),
                vm(3, cx + 1, cy, nz),
                vm(3, cx + 1, ROWS, nz),
                vm(3, cx + 1, cy, nz),
                vm(SECTIONS, wide, ROWS, nz),
                vm(phases, 2, cx, nz),
                vm(phases, 3, cx, nz),
                vm(phases, 3, cx, nz),
                pltpu.SemaphoreType.DMA((SECTIONS, 8)),
                pltpu.SemaphoreType.DMA((SECTIONS, 8)),
            ],
            compiler_params=pltpu.CompilerParams(collective_id=0, has_side_effects=True),
        )(rho, v, p, b)

    placed = (
        P("gx", "gy", None),
        P(None, "gx", "gy", None),
        P("gx", "gy", None),
        P(None, "gx", "gy", None),
    )
    return jax.shard_map(
        lambda *a: tuple(local(*a)),
        mesh=mesh,
        in_specs=placed,
        out_specs=placed,
        check_vma=False,
    )
```

time: 92.4 us -> 42 us (0.45)
  Pallas kernels: 0 us -> 36.9 us
  starting transfers between devices: 34.5 us -> 0 us
  waiting for transfers between devices: 23.8 us -> 0 us
  other arithmetic: 15 us -> 0 us
  local copies, waits for them, and re-layouts: 16 us -> 4.21 us
  between operations: 2.72 us -> 0.64 us
    pallas_call x0 -> x1, Pallas kernels: none -> 36.9 us  [local(): pl.pallas_call(functools.partial(kernel, nx, ny), out_shape=[jax.ShapeDty...]
    ppermute x20 -> x0, starting transfers between devices: 34.5 us -> none  [the longest x10 27.8 us: extended_2(): lax.ppermute(lax.slice_in_dim(block, 0, width, axis=dim), axis, backward)]
    ppermute x20 -> x0, waiting for transfers between devices: 23.8 us -> none  [the longest x10 18.9 us: extended_2(): lax.ppermute(lax.slice_in_dim(block, block.shape[dim] - width, None, axis...]
    sub x19 -> x0, other arithmetic: 6.79 us -> none  [the longest x17 6.48 us: face_fluxes(): 0.5 * (flux_lower[n] + flux_upper[n])]
    slice x212 -> x0, local copies, waits for them, and re-layouts: 6.31 us -> none  [the longest x207 6.22 us: adjacent_zone(): return jnp.roll(a, -k, dimension)]
    unnamed x39 -> x8, local copies, waits for them, and re-layouts: 9.62 us -> 4.21 us
    mul x24 -> x0, other arithmetic: 2.47 us -> none  [the longest x12 0.81 us: conduction(): 0.5 * (adjacent_zone(plasma_thermal_level, zone_quantities, 1) - adjacent...]
    add x11 -> x0, other arithmetic: 2.27 us -> none  [the longest x6 1.55 us: face_fluxes(): quantity + 0.5 * gradient]
  transfers between devices with their start and end apart: 20 -> 0, of which waited for: 11 -> 0; matrix products, arithmetic and copies ran while one was open for 1% -> 0% of each run, Pallas kernels for 0% -> 0%
where the time goes in v1:
time: 42 us; the launch traced here: 41.8 us
  Pallas kernels  36.9 us (88%)
  local copies, waits for them, and re-layouts  4.21 us (10%)
  between operations  0.64 us (2%)
    pallas_call x1, Pallas kernels, local(): pl.pallas_call(functools.partial(kernel, nx, ny), out_shape=[jax.ShapeDty...  36.9 us
    unnamed x8, local copies, waits for them, and re-layouts  4.21 us

profile of v1, /device:TPU:0, one launch (start us, length us, event | category | flops | bytes accessed | tf_op | source)
XLA Modules:
  0.0 41.8 jit_solution(2274429252319058805)
XLA Ops:
  0.6 36.9 %shard_map.75 = (f32[8,8,128]{2,1,0:T(8,128)}, f32[3,8,8,128]{3,2,1,0:T(8,128)}, f32[8,8,128]{2,1,0:T(8,128)}, f32[3,8,8,128]{3,2,1,0:T(8,128)}) custom-call(f32[8,8,128]{2,1,0:T(8,128)} %rho_ref.1, f32[3,8,8,128]{3,2,1,0:T(8,128)} %v_ref.1, f32[8,8,128]{2,1,0:T(8,128)} %p_ref.1, f32[3,8,8,128]{3,2,1,0:T(8,128)} %b_ref.1), custom_call_target="tpu_custom_call" | custom-call | tf_op jit(solution)/shard_map/pallas_call | solution.py:377
  37.6 1.4 %copy.12 = f32[8,8,128]{2,1,0:T(8,128)} copy(f32[8,8,128]{2,1,0:T(8,128)} %get-tuple-element.8) | data formatting | bytes 65536
  38.9 0.0 copy-start.1
  38.9 0.0 copy-start
  38.9 1.6 %copy.13 = f32[3,8,8,128]{3,2,1,0:T(8,128)} copy(f32[3,8,8,128]{3,2,1,0:T(8,128)} %get-tuple-element.9) | data formatting | bytes 196608
  40.5 0.0 copy-done.1
  40.5 0.6 %copy.14 = f32[8,8,128]{2,1,0:T(8,128)} copy(f32[8,8,128]{2,1,0:T(8,128)S(1)} %copy-done.1) | data formatting | bytes 65536
  41.1 0.0 copy-done
  41.1 0.6 %copy.15 = f32[3,8,8,128]{3,2,1,0:T(8,128)} copy(f32[3,8,8,128]{3,2,1,0:T(8,128)S(1)} %copy-done) | data formatting | bytes 196608
Async XLA Ops:
  38.9 1.6 %copy-start.1 = (f32[8,8,128]{2,1,0:T(8,128)S(1)}, f32[8,8,128]{2,1,0:T(8,128)}, u32[]{:S(2)}) copy-start(f32[8,8,128]{2,1,0:T(8,128)} %get-tuple-element.10) | copy-start | bytes 98308
  38.9 2.2 %copy-start = (f32[3,8,8,128]{3,2,1,0:T(8,128)S(1)}, f32[3,8,8,128]{3,2,1,0:T(8,128)}, u32[]{:S(2)}) copy-start(f32[3,8,8,128]{3,2,1,0:T(8,128)} %get-tuple-element.11) | copy-start | bytes 294916

commit v2 on v1

--- a/solution.py
+++ b/solution.py
@@ -105,15 +105,15 @@
 def kernel(
     nx, ny,
     rho_ref, v_ref, p_ref, b_ref,
+    rho_out, v_out, p_out, b_out,
     o_rho, o_v, o_p, o_b,
     ext, up, down, from_low, from_high,
     lower_s, diff_s, cell_s, d_s, f_s, b_s,
     irho_s, e_s, kap_s, bc_s, bf_s, kx_s, ky_s, kz_s,
     t_s, pk, low_row, high_row,
-    send_sem, recv_sem,
+    send_sem, recv_sem, in_sem, out_sem,
 ):
-    cx = rho_ref.shape[0]
-    cy = rho_ref.shape[1]
+    cx, cy = o_rho.shape[0], o_rho.shape[1]
     gx, gy = lax.axis_index("gx"), lax.axis_index("gy")
 
     def target(dx, dy):
@@ -125,12 +125,24 @@
     for dx, dy in ring:
         pl.semaphore_signal(barrier, inc=1, device_id=target(dx, dy), device_id_type=MESH)
 
-    fields = [rho_ref] + [v_ref.at[c] for c in range(3)] + [p_ref] + [b_ref.at[c] for c in range(3)]
-    for f, ref in enumerate(fields):
-        value = ref[...]
+    own, near = pl.ds(H, cx), pl.ds(0, cy)
+    places = [
+        (rho_ref, ext.at[0, own, near]),
+        (v_ref, ext.at[pl.ds(1, 3), own, near]),
+        (p_ref, ext.at[4, own, near]),
+        (b_ref, ext.at[pl.ds(5, 3), own, near]),
+    ]
+    loads = [
+        pltpu.make_async_copy(src, dst, in_sem.at[n]) for n, (src, dst) in enumerate(places)
+    ]
+    for load in loads:
+        load.start()
+    for load in loads:
+        load.wait()
+    for f in range(8):
+        value = ext[f, H : H + cx, 0:cy, :]
         up[:, H * f : H * f + H, :] = value[:, cy - H : cy, :]
         down[:, H * f : H * f + H, :] = value[:, 0:H, :]
-        ext[f, H : H + cx, 0:cy, :] = value
     pl.semaphore_wait(barrier, len(ring))
 
     def remote(phase, k, src, dst):
@@ -169,12 +181,14 @@
     for ref in (lower_s, diff_s, cell_s, d_s, f_s, b_s):
         for n in range(ref.shape[0]):
             ref[n] = one
+    for f in range(8):
+        ext[f, :, cy:ROWS, :] = jnp.ones((cx + 2 * H, ROWS - cy, 128), jnp.float32)
+    sent = list(copies)
     for copy in copies:
-        copy.wait()
+        copy.wait_recv()
 
     def unpack(s, carry):
         for f in range(8):
-            ext[f, s, cy:ROWS, :] = jnp.ones((ROWS - cy, 128), jnp.float32)
             ext[f, s, cy : cy + H, :] = from_high[s, H * f : H * f + H, :]
             ext[f, s, ROWS - H : ROWS, :] = from_low[s, H * f : H * f + H, :]
         return carry
@@ -266,7 +280,13 @@
 
         return carry
 
-    lax.fori_loop(1, cx + 2 * H - 1, body, 0)
+    lax.fori_loop(1, cx + 2 * H - 1, body, 0, unroll=2)
+    stores = [
+        pltpu.make_async_copy(src, dst, out_sem.at[n])
+        for n, (src, dst) in enumerate(((o_rho, rho_out), (o_v, v_out), (o_b, b_out)))
+    ]
+    for store in stores:
+        store.start()
 
     def coupling(s, carry):
         kap = kap_s[s]
@@ -349,8 +369,9 @@
                     )
                 )
         part = mu * latest + nu * earlier + rest * base + zero * rate0
+        sent += copies
         for copy in copies:
-            copy.wait()
+            copy.wait_recv()
         for s in range(cx + 2):
             if s == 0:
                 d, x = 2, cx - 1
@@ -362,6 +383,22 @@
             t_s[phase, H - 1 + s, ROWS - 1 : ROWS, :] = low_row[n, d, x : x + 1, :]
         earlier, latest = latest, part + fresh * rate(phase)
     o_p[...] = (G - 1.0) * latest
+    stores.append(pltpu.make_async_copy(o_p, p_out, out_sem.at[3]))
+    stores[3].start()
+    for copy in sent:
+        copy.wait_send()
+    for store in stores:
+        store.wait()
+
+
+def hand_on(*refs):
+    copies = [
+        pltpu.make_async_copy(refs[n], refs[4 + n], refs[8].at[n]) for n in range(4)
+    ]
+    for copy in copies:
+        copy.start()
+    for copy in copies:
+        copy.wait()
 
 
 def solution(mesh):
@@ -373,18 +410,18 @@
         f32 = jnp.float32
         vm = lambda *shape: pltpu.VMEM(shape, f32)
         phases = SECTIONS - 1
-        spec = pl.BlockSpec(memory_space=pltpu.VMEM)
-        return pl.pallas_call(
+        spec = pl.BlockSpec(memory_space=pl.ANY)
+        shapes = [jax.ShapeDtypeStruct(a.shape, f32) for a in (rho, v, p, b)]
+        results = pl.pallas_call(
             functools.partial(kernel, nx, ny),
-            out_shape=[
-                jax.ShapeDtypeStruct(rho.shape, f32),
-                jax.ShapeDtypeStruct(v.shape, f32),
-                jax.ShapeDtypeStruct(p.shape, f32),
-                jax.ShapeDtypeStruct(b.shape, f32),
-            ],
-            in_specs=[spec] * 4,
+            out_shape=shapes,
+            in_specs=[pl.BlockSpec(memory_space=pltpu.HBM)] * 4,
             out_specs=[spec] * 4,
             scratch_shapes=[
+                vm(cx, cy, nz),
+                vm(3, cx, cy, nz),
+                vm(cx, cy, nz),
+                vm(3, cx, cy, nz),
                 vm(8, wide, ROWS, nz),
                 vm(cx, 8 * H, nz),
                 vm(cx, 8 * H, nz),
@@ -410,9 +447,18 @@
                 vm(phases, 3, cx, nz),
                 pltpu.SemaphoreType.DMA((SECTIONS, 8)),
                 pltpu.SemaphoreType.DMA((SECTIONS, 8)),
+                pltpu.SemaphoreType.DMA((4,)),
+                pltpu.SemaphoreType.DMA((4,)),
             ],
             compiler_params=pltpu.CompilerParams(collective_id=0, has_side_effects=True),
         )(rho, v, p, b)
+        return pl.pallas_call(
+            hand_on,
+            out_shape=shapes,
+            in_specs=[spec] * 4,
+            out_specs=[spec] * 4,
+            scratch_shapes=[pltpu.SemaphoreType.DMA((4,))],
+        )(*results)
 
     placed = (
         P("gx", "gy", None),

time: 42 us -> 45.9 us (1.093)
  Pallas kernels: 36.9 us -> 45.1 us
  local copies, waits for them, and re-layouts: 4.21 us -> 0 us
    pallas_call x1 -> x2, Pallas kernels: 36.9 us -> 45.1 us  [the longest x1 36 us: local(): pl.pallas_call(functools.partial(kernel, nx, ny), out_shape=shapes, in_sp...]
    unnamed x8 -> x0, local copies, waits for them, and re-layouts: 4.21 us -> none
where the time goes in v2:
time: 45.9 us; the launch traced here: 45.8 us
  Pallas kernels  45.1 us (98%)
  between operations  0.64 us (1%)
    pallas_call x1, Pallas kernels, local(): pl.pallas_call(functools.partial(kernel, nx, ny), out_shape=shapes, in_sp...  36 us
    pallas_call x1, Pallas kernels, local(): pl.pallas_call(hand_on, out_shape=shapes, in_specs=[spec] * 4, out_specs=...  9.08 us

profile of v2, /device:TPU:0, one launch (start us, length us, event | category | flops | bytes accessed | tf_op | source)
XLA Modules:
  0.0 45.8 jit_solution(2601595882726426530)
XLA Ops:
  0.6 36.0 %shard_map.75 = (f32[8,8,128]{2,1,0:T(8,128)}, f32[3,8,8,128]{3,2,1,0:T(8,128)}, f32[8,8,128]{2,1,0:T(8,128)}, f32[3,8,8,128]{3,2,1,0:T(8,128)}) custom-call(f32[8,8,128]{2,1,0:T(8,128)} %rho_ref.1, f32[3,8,8,128]{3,2,1,0:T(8,128)} %v_ref.1, f32[8,8,128]{2,1,0:T(8,128)} %p_ref.1, f32[3,8,8,128]{3,2,1,0:T(8,128)} %b_ref.1), custom_call_target="tpu_custom_call" | custom-call | tf_op jit(solution)/shard_map/pallas_call | solution.py:415
  36.7 9.1 %shard_map.76 = (f32[8,8,128]{2,1,0:T(8,128)}, f32[3,8,8,128]{3,2,1,0:T(8,128)}, f32[8,8,128]{2,1,0:T(8,128)}, f32[3,8,8,128]{3,2,1,0:T(8,128)}) custom-call(f32[8,8,128]{2,1,0:T(8,128)} %get-tuple-element.8.refs_0_, f32[3,8,8,128]{3,2,1,0:T(8,128)} %get-tuple-element.9.refs_1_, f32[8,8,128]{2,1,0:T(8,128)} %get-tuple-element.10.refs_2_, ...), custom_call_target="tpu_custom_call" | custom-call | tf_op jit(solution)/shard_map/pallas_call | solution.py:455

commit v3 on v2

--- a/solution.py
+++ b/solution.py
@@ -108,7 +108,7 @@
     rho_out, v_out, p_out, b_out,
     o_rho, o_v, o_p, o_b,
     ext, up, down, from_low, from_high,
-    lower_s, diff_s, cell_s, d_s, f_s, b_s,
+    cell, fx_s, fy_s, fz_s, b_s,
     irho_s, e_s, kap_s, bc_s, bf_s, kx_s, ky_s, kz_s,
     t_s, pk, low_row, high_row,
     send_sem, recv_sem, in_sem, out_sem,
@@ -145,93 +145,148 @@
         down[:, H * f : H * f + H, :] = value[:, 0:H, :]
     pl.semaphore_wait(barrier, len(ring))
 
-    def remote(phase, k, src, dst):
+    def remote(phase, k, src, dst, to=None):
         copy = pltpu.make_async_remote_copy(
             src_ref=src,
             dst_ref=dst,
             send_sem=send_sem.at[phase, k],
             recv_sem=recv_sem.at[phase, k],
-            device_id=target(*ring[k]),
+            device_id=target(*(to or ring[k])),
             device_id_type=MESH,
         )
         copy.start()
         return copy
 
-    copies = []
-    for k, (dx, dy) in enumerate(ring):
-        if dx == 0:
-            here, there = slice(0, cx), slice(H, H + cx)
-        elif dx == 1:
-            here, there = slice(cx - H, cx), slice(0, H)
-        else:
-            here, there = slice(0, H), slice(H + cx, 2 * H + cx)
-        here = pl.ds(here.start, here.stop - here.start)
-        there = pl.ds(there.start, there.stop - there.start)
-        if dy == 1:
-            copies.append(remote(0, k, up.at[here], from_low.at[there]))
-        elif dy == -1:
-            copies.append(remote(0, k, down.at[here], from_high.at[there]))
-        else:
-            src = pl.ds(here.start + H, here.size)
-            copies.append(
-                remote(0, k, ext.at[:, src, pl.ds(0, cy)], ext.at[:, there, pl.ds(0, cy)])
-            )
+    def side(k):
+        return ring.index(k)
+
+    wide = cx + 2 * H
+    mine, low3, high3 = pl.ds(H, cx), pl.ds(0, H), pl.ds(H + cx, H)
+    first3, last3 = pl.ds(H, H), pl.ds(cx, H)
+
+    to_high = remote(0, side((0, 1)), up, from_low.at[mine])
+    to_low = remote(0, side((0, -1)), down, from_high.at[mine])
+    slabs = [
+        remote(0, side((1, 0)), ext.at[:, last3, near], ext.at[:, low3, near]),
+        remote(0, side((-1, 0)), ext.at[:, first3, near], ext.at[:, high3, near]),
+    ]
+    sent = [to_high, to_low] + slabs
 
     one = jnp.ones((ROWS, 128), jnp.float32)
-    for ref in (lower_s, diff_s, cell_s, d_s, f_s, b_s):
-        for n in range(ref.shape[0]):
-            ref[n] = one
+    for n in range(3):
+        b_s[n] = one
     for f in range(8):
-        ext[f, :, cy:ROWS, :] = jnp.ones((cx + 2 * H, ROWS - cy, 128), jnp.float32)
-    sent = list(copies)
-    for copy in copies:
+        ext[f, :, cy:ROWS, :] = jnp.ones((wide, ROWS - cy, 128), jnp.float32)
+
+    A, B, BOTH = slice(0, cy), slice(cy, ROWS), slice(0, ROWS)
+
+    def cells_own(s, e):
+        bx, by, bz = (ext[5 + c, s:e, A] for c in range(3))
+        nx_, nz_ = ext[5, s + 1 : e + 1, A], pltpu.roll(bz, 127, 2)
+        cell[0, s:e, A] = 0.5 * (bx + nx_)
+        cell[1, s:e, A] = by - 0.5 * ((nx_ - bx) + (nz_ - bz))
+        cell[2, s:e, A] = 0.5 * (bz + nz_)
+
+    def cell_x(s, e):
+        cell[0, s:e, B] = 0.5 * (ext[5, s:e, B] + ext[5, s + 1 : e + 1, B])
+
+    def cell_yz(s, e, rows):
+        for x in range(s, e):
+            by, bz = ext[6, x], ext[7, x, rows]
+            cell[1, x, rows] = (0.5 * (by + yhigh(by)))[rows]
+            cell[2, x, rows] = 0.5 * (bz + zhigh(bz))
+
+    def prims(s, rows, d):
+        return [ext[f, s, rows] for f in range(5)] + [
+            cell[c, s, rows] for c in range(3) if c != d
+        ]
+
+    def flux_z(s, rows):
+        for n, a in enumerate(along(prims(s, rows, 2), ext[7, s, rows], 2)):
+            fz_s[n, s, rows] = a
+
+    def flux_y(s):
+        for n, a in enumerate(along(prims(s, BOTH, 1), ext[6, s], 1)):
+            fy_s[n, s] = a
+
+    def flux_x(i, rows):
+        q = [prims(i + o, rows, 0) for o in (-2, -1, 0, 1)]
+        lower, upper = [], []
+        for q0, q1, q2, q3 in zip(*q):
+            d1 = q2 - q1
+            lower.append(q1 + 0.5 * minmod(q1 - q0, d1))
+            upper.append(q2 - 0.5 * minmod(d1, q3 - q2))
+        for n, a in enumerate(face_flux(lower, upper, ext[5, i, rows], 0)):
+            fx_s[n, i, rows] = a
+
+    def loop(count, f, unroll):
+        def step(k, carry):
+            f(k)
+            return carry
+
+        lax.fori_loop(0, count, step, 0, unroll=unroll)
+
+    def outer(k):
+        return k + 1 + (cx - 1) * ((k + 3) // 5)
+
+    cells_own(H, H + cx - 1)
+    loop(cx - 1, lambda k: flux_z(H + k, A), cx - 1)
+    for copy in slabs:
         copy.wait_recv()
-
-    def unpack(s, carry):
+    cells_own(0, H)
+    cells_own(H + cx - 1, wide - 1)
+    loop(5, lambda k: flux_z(outer(k), A), 5)
+    loop(cx + 2, lambda k: flux_x(2 + k, A), 2)
+
+    corners = []
+    for copy, dy, buffer in ((to_high, 1, from_low), (to_low, -1, from_high)):
+        copy.wait_recv()
+        corners.append(remote(0, side((1, dy)), buffer.at[last3], buffer.at[low3], (1, 0)))
+        corners.append(remote(0, side((-1, dy)), buffer.at[first3], buffer.at[high3], (-1, 0)))
+    sent += corners
+
+    def unpack(s, e):
         for f in range(8):
-            ext[f, s, cy : cy + H, :] = from_high[s, H * f : H * f + H, :]
-            ext[f, s, ROWS - H : ROWS, :] = from_low[s, H * f : H * f + H, :]
-        return carry
-
-    lax.fori_loop(0, cx + 2 * H, unpack, 0)
-
-    def cells(s):
-        by, bz = ext[6, s], ext[7, s]
-        return [0.5 * (by + yhigh(by)), 0.5 * (bz + zhigh(bz))]
-
-    def raw(s):
-        return [ext[f, s] for f in range(5)] + cells(s)
-
-    first, second = raw(0), raw(1)
-    for n in range(7):
-        diff_s[n] = second[n] - first[n]
-    cell_s[0] = second[5]
-    cell_s[1] = second[6]
-
-    def body(i, carry):
-        here = [ext[f, i] for f in range(5)] + [cell_s[0], cell_s[1]]
-        there = raw(i + 1)
+            ext[f, s:e, cy : cy + H, :] = from_high[s:e, H * f : H * f + H, :]
+            ext[f, s:e, ROWS - H : ROWS, :] = from_low[s:e, H * f : H * f + H, :]
+
+    unpack(H, H + cx)
+    cell_x(H, H + cx - 1)
+    cell_yz(H, H + cx, B)
+
+    def middle(k):
+        flux_y(H + k)
+        flux_z(H + k, B)
+
+    loop(cx - 1, middle, 1)
+    loop(cx - 3, lambda k: flux_x(H + 2 + k, B), cx - 3)
+
+    for copy in corners:
+        copy.wait_recv()
+    unpack(0, H)
+    unpack(H + cx, wide)
+    cell_x(0, H)
+    cell_x(H + cx - 1, wide - 1)
+    cell_yz(0, H, B)
+    cell_yz(H + cx, wide - 1, B)
+    cell_yz(wide - 1, wide, BOTH)
+
+    def ends(k):
+        flux_y(outer(k))
+        flux_z(outer(k), B)
+
+    loop(5, ends, 1)
+    loop(6, lambda k: flux_x(2 + k + (cx - 3) * (k // 3), B), 2)
+    flux_x(wide - 2, A)
+
+    def body(i):
         bx, by, bz = ext[5, i], ext[6, i], ext[7, i]
-        cell = [0.5 * (bx + ext[5, i + 1]), here[5], here[6]]
-        lower = [lower_s[n] for n in range(7)]
-        upper = []
-        for n in range(7):
-            diff = there[n] - here[n]
-            half = 0.5 * minmod(diff_s[n], diff)
-            diff_s[n] = diff
-            upper.append(here[n] - half)
-            lower_s[n] = here[n] + half
-        cell_s[0] = there[5]
-        cell_s[1] = there[6]
-        fx = face_flux(lower, upper, bx, 0)
-        fy = along(here[:5] + [cell[0], cell[2]], by, 1)
-        fz = along(here[:5] + [cell[0], cell[1]], bz, 2)
-
-        ez = 0.25 * (f_s[0] + fy[5] - ylow(fx[5]) - fx[5])
-        ey = 0.25 * (zlow(fx[6]) + fx[6] - f_s[1] - fz[5])
-        ex = 0.25 * (ylow(fz[6]) + fz[6] - zlow(fy[6]) - fy[6])
-        f_s[0] = fy[5]
-        f_s[1] = fz[5]
+        xy, xz = fx_s[5, i], fx_s[6, i]
+        yx, yz = fy_s[5, i], fy_s[6, i]
+        zx, zy = fz_s[5, i], fz_s[6, i]
+        ez = 0.25 * (fy_s[5, i - 1] + yx - ylow(xy) - xy)
+        ey = 0.25 * (zlow(xz) + xz - fz_s[5, i - 1] - zx)
+        ex = 0.25 * (ylow(zy) + zy - zlow(yz) - yz)
         bxn = bx - DT * (yhigh(ez) - ez) + DT * (zhigh(ey) - ey)
         bxo = b_s[0]
         byn = b_s[1] + DT * ez
@@ -240,18 +295,20 @@
         b_s[1] = by - DT * (zhigh(ex) - ex) - DT * ez
         b_s[2] = bz + DT * ey + DT * (yhigh(ex) - ex)
 
-        rho, v, p = here[0], here[1:4], here[4]
+        m = i - 1
+        rho, v, p = ext[0, m], [ext[1 + c, m] for c in range(3)], ext[4, m]
+        bm = [cell[c, m] for c in range(3)]
         energy = (
             p * 1.5
             + 0.5 * rho * (v[0] * v[0] + v[1] * v[1] + v[2] * v[2])
-            + 0.5 * (cell[0] * cell[0] + cell[1] * cell[1] + cell[2] * cell[2])
+            + 0.5 * (bm[0] * bm[0] + bm[1] * bm[1] + bm[2] * bm[2])
         )
-        cons = [rho, rho * v[0], rho * v[1], rho * v[2], energy]
-        new = [d_s[n] - DT * fx[n] for n in range(5)]
+        new = [rho, rho * v[0], rho * v[1], rho * v[2], energy]
         for n in range(5):
-            d_s[n] = cons[n] - DT * ((yhigh(fy[n]) - fy[n]) + (zhigh(fz[n]) - fz[n]) - fx[n])
-
-        m = i - 1
+            fy, fz = fy_s[n, m], fz_s[n, m]
+            change = (yhigh(fy) - fy) + (zhigh(fz) - fz) + (fx_s[n, i] - fx_s[n, m])
+            new[n] = new[n] - DT * change
+
         floored = jnp.maximum(new[0], DENSITY_FLOOR)
         inv = 1.0 / floored
         vel = [new[1 + c] * inv for c in range(3)]
@@ -268,19 +325,17 @@
             bc_s[c, m] = bc[c]
         for c, a in enumerate((bxo, byn, bzn)):
             bf_s[c, m] = a
-
-        @pl.when(jnp.logical_and(m >= H, m < H + cx))
-        def _():
-            x = jnp.clip(m - H, 0, cx - 1)
-            o_rho[x] = floored[0:cy]
-            for c in range(3):
-                o_v[c, x] = vel[c][0:cy]
-            for c, a in enumerate((bxo, byn, bzn)):
-                o_b[c, x] = a[0:cy]
-
-        return carry
-
-    lax.fori_loop(1, cx + 2 * H - 1, body, 0, unroll=2)
+        if isinstance(i, int):
+            return
+        x = jnp.maximum(m - H, 0)
+        o_rho[x] = floored[A]
+        for c in range(3):
+            o_v[c, x] = vel[c][A]
+        for c, a in enumerate((bxo, byn, bzn)):
+            o_b[c, x] = a[A]
+
+    loop(cx + 2, lambda k: body(2 + k), 2)
+    body(wide - 2)
     stores = [
         pltpu.make_async_copy(src, dst, out_sem.at[n])
         for n, (src, dst) in enumerate(((o_rho, rho_out), (o_v, v_out), (o_b, b_out)))
@@ -307,7 +362,7 @@
                 out[c, s - H] = k[0:rows]
         return carry
 
-    lax.fori_loop(H, H + cx + 1, coupling, 0)
+    lax.fori_loop(H, H + cx + 1, coupling, 0, unroll=3)
 
     def rate(phase):
         t = [t_s[phase, H - 1 + s] for s in range(cx + 2)]
@@ -392,13 +447,16 @@
 
 
 def hand_on(*refs):
-    copies = [
-        pltpu.make_async_copy(refs[n], refs[4 + n], refs[8].at[n]) for n in range(4)
-    ]
-    for copy in copies:
-        copy.start()
-    for copy in copies:
-        copy.wait()
+    source, result, held, in_sem, out_sem = refs[:4], refs[4:8], refs[8:12], refs[12], refs[13]
+    loads = [pltpu.make_async_copy(source[n], held[n], in_sem.at[n]) for n in range(4)]
+    stores = [pltpu.make_async_copy(held[n], result[n], out_sem.at[n]) for n in range(4)]
+    for load in loads:
+        load.start()
+    for load, store in zip(loads, stores):
+        load.wait()
+        store.start()
+    for store in stores:
+        store.wait()
 
 
 def solution(mesh):
@@ -427,11 +485,10 @@
                 vm(cx, 8 * H, nz),
                 vm(wide, 8 * H, nz),
                 vm(wide, 8 * H, nz),
-                vm(7, ROWS, nz),
-                vm(7, ROWS, nz),
-                vm(2, ROWS, nz),
-                vm(5, ROWS, nz),
-                vm(2, ROWS, nz),
+                vm(3, wide, ROWS, nz),
+                vm(7, wide, ROWS, nz),
+                vm(7, wide, ROWS, nz),
+                vm(7, wide, ROWS, nz),
                 vm(3, ROWS, nz),
                 vm(wide, ROWS, nz),
                 vm(wide, ROWS, nz),
@@ -457,7 +514,8 @@
             out_shape=shapes,
             in_specs=[spec] * 4,
             out_specs=[spec] * 4,
-            scratch_shapes=[pltpu.SemaphoreType.DMA((4,))],
+            scratch_shapes=[vm(*a.shape) for a in shapes]
+            + [pltpu.SemaphoreType.DMA((4,)), pltpu.SemaphoreType.DMA((4,))],
         )(*results)
 
     placed = (

time: 45.9 us -> 35.8 us (0.78)
  Pallas kernels: 45.1 us -> 34.9 us
    pallas_call x1, Pallas kernels: 9.08 us -> 1.69 us  [local(): pl.pallas_call(hand_on, out_shape=shapes, in_specs=[spec] * 4, out_specs=...]
    pallas_call x1, Pallas kernels: 36 us -> 33.2 us  [local(): pl.pallas_call(functools.partial(kernel, nx, ny), out_shape=shapes, in_sp...]
where the time goes in v3:
time: 35.8 us; the launch traced here: 35.6 us
  Pallas kernels  34.9 us (97%)
  between operations  0.64 us (2%)
    pallas_call x1, Pallas kernels, local(): pl.pallas_call(functools.partial(kernel, nx, ny), out_shape=shapes, in_sp...  33.2 us
    pallas_call x1, Pallas kernels, local(): pl.pallas_call(hand_on, out_shape=shapes, in_specs=[spec] * 4, out_specs=...  1.69 us

profile of v3, /device:TPU:0, one launch (start us, length us, event | category | flops | bytes accessed | tf_op | source)
XLA Modules:
  0.0 35.6 jit_solution(8723396039758770995)
XLA Ops:
  0.6 33.2 %shard_map.75 = (f32[8,8,128]{2,1,0:T(8,128)}, f32[3,8,8,128]{3,2,1,0:T(8,128)}, f32[8,8,128]{2,1,0:T(8,128)}, f32[3,8,8,128]{3,2,1,0:T(8,128)}) custom-call(f32[8,8,128]{2,1,0:T(8,128)} %rho_ref.1, f32[3,8,8,128]{3,2,1,0:T(8,128)} %v_ref.1, f32[8,8,128]{2,1,0:T(8,128)} %p_ref.1, f32[3,8,8,128]{3,2,1,0:T(8,128)} %b_ref.1), custom_call_target="tpu_custom_call" | custom-call | tf_op jit(solution)/shard_map/pallas_call | solution.py:473
  33.9 1.7 %shard_map.76 = (f32[8,8,128]{2,1,0:T(8,128)}, f32[3,8,8,128]{3,2,1,0:T(8,128)}, f32[8,8,128]{2,1,0:T(8,128)}, f32[3,8,8,128]{3,2,1,0:T(8,128)}) custom-call(f32[8,8,128]{2,1,0:T(8,128)} %get-tuple-element.8.refs_0_, f32[3,8,8,128]{3,2,1,0:T(8,128)} %get-tuple-element.9.refs_1_, f32[8,8,128]{2,1,0:T(8,128)} %get-tuple-element.10.refs_2_, ...), custom_call_target="tpu_custom_call" | custom-call | tf_op jit(solution)/shard_map/pallas_call | solution.py:512

commit v4 on v3

--- a/solution.py
+++ b/solution.py
@@ -19,7 +19,7 @@
 
 MESH = pl.DeviceIdType.MESH
 
-H = 3
+H = 4
 ROWS = 16
 
 
@@ -109,8 +109,8 @@
     o_rho, o_v, o_p, o_b,
     ext, up, down, from_low, from_high,
     cell, fx_s, fy_s, fz_s, b_s,
-    irho_s, e_s, kap_s, bc_s, bf_s, kx_s, ky_s, kz_s,
-    t_s, pk, low_row, high_row,
+    irho_s, kap_s, bc_s, bf_s, kx_s, ky_s, kz_s,
+    t_s, r_s, pk, low_row, high_row,
     send_sem, recv_sem, in_sem, out_sem,
 ):
     cx, cy = o_rho.shape[0], o_rho.shape[1]
@@ -161,22 +161,20 @@
         return ring.index(k)
 
     wide = cx + 2 * H
-    mine, low3, high3 = pl.ds(H, cx), pl.ds(0, H), pl.ds(H + cx, H)
-    first3, last3 = pl.ds(H, H), pl.ds(cx, H)
+    mine, low_h, high_h = pl.ds(H, cx), pl.ds(0, H), pl.ds(H + cx, H)
+    first_h, last_h = pl.ds(H, H), pl.ds(cx, H)
 
     to_high = remote(0, side((0, 1)), up, from_low.at[mine])
     to_low = remote(0, side((0, -1)), down, from_high.at[mine])
     slabs = [
-        remote(0, side((1, 0)), ext.at[:, last3, near], ext.at[:, low3, near]),
-        remote(0, side((-1, 0)), ext.at[:, first3, near], ext.at[:, high3, near]),
+        remote(0, side((1, 0)), ext.at[:, last_h, near], ext.at[:, low_h, near]),
+        remote(0, side((-1, 0)), ext.at[:, first_h, near], ext.at[:, high_h, near]),
     ]
     sent = [to_high, to_low] + slabs
 
     one = jnp.ones((ROWS, 128), jnp.float32)
     for n in range(3):
         b_s[n] = one
-    for f in range(8):
-        ext[f, :, cy:ROWS, :] = jnp.ones((wide, ROWS - cy, 128), jnp.float32)
 
     A, B, BOTH = slice(0, cy), slice(cy, ROWS), slice(0, ROWS)
 
@@ -227,7 +225,7 @@
         lax.fori_loop(0, count, step, 0, unroll=unroll)
 
     def outer(k):
-        return k + 1 + (cx - 1) * ((k + 3) // 5)
+        return k + 1 + (cx - 1) * ((k + cx - H) // (cx - 1))
 
     cells_own(H, H + cx - 1)
     loop(cx - 1, lambda k: flux_z(H + k, A), cx - 1)
@@ -235,14 +233,14 @@
         copy.wait_recv()
     cells_own(0, H)
     cells_own(H + cx - 1, wide - 1)
-    loop(5, lambda k: flux_z(outer(k), A), 5)
-    loop(cx + 2, lambda k: flux_x(2 + k, A), 2)
+    loop(cx - 1, lambda k: flux_z(outer(k), A), cx - 1)
+    loop(cx + 4, lambda k: flux_x(2 + k, A), 2)
 
     corners = []
     for copy, dy, buffer in ((to_high, 1, from_low), (to_low, -1, from_high)):
         copy.wait_recv()
-        corners.append(remote(0, side((1, dy)), buffer.at[last3], buffer.at[low3], (1, 0)))
-        corners.append(remote(0, side((-1, dy)), buffer.at[first3], buffer.at[high3], (-1, 0)))
+        corners.append(remote(0, side((1, dy)), buffer.at[last_h], buffer.at[low_h], (1, 0)))
+        corners.append(remote(0, side((-1, dy)), buffer.at[first_h], buffer.at[high_h], (-1, 0)))
     sent += corners
 
     def unpack(s, e):
@@ -275,8 +273,8 @@
         flux_y(outer(k))
         flux_z(outer(k), B)
 
-    loop(5, ends, 1)
-    loop(6, lambda k: flux_x(2 + k + (cx - 3) * (k // 3), B), 2)
+    loop(cx - 1, ends, 1)
+    loop(2 * H, lambda k: flux_x(2 + k + (cx - 3) * (k // H), B), 2)
     flux_x(wide - 2, A)
 
     def body(i):
@@ -318,7 +316,6 @@
         p1 = jnp.maximum((G - 1.0) * internal, PRESSURE_FLOOR)
         t = p1 * inv
         irho_s[m] = (G - 1.0) * inv
-        e_s[m] = p1 * 1.5
         t_s[0, m] = t
         kap_s[m] = t * t * jnp.sqrt(t)
         for c in range(3):
@@ -334,7 +331,9 @@
         for c, a in enumerate((bxo, byn, bzn)):
             o_b[c, x] = a[A]
 
-    loop(cx + 2, lambda k: body(2 + k), 2)
+    body(2)
+    loop(cx + 2, lambda k: body(3 + k), 2)
+    body(wide - 3)
     body(wide - 2)
     stores = [
         pltpu.make_async_copy(src, dst, out_sem.at[n])
@@ -356,88 +355,94 @@
             comp = [bf[d] if c == d else 0.5 * (bc[c] + bl[c]) for c in range(3)]
             mag = comp[0] * comp[0] + comp[1] * comp[1] + comp[2] * comp[2]
             factor = 0.5 * (kap + kl) / jnp.maximum(mag, FIELD_FLOOR) * bf[d]
-            rows = ROWS if d == 1 else cy
             for c in range(3):
-                k = factor * comp[c] * (1.0 if c == d else 0.25)
-                out[c, s - H] = k[0:rows]
+                out[c, s - H + 1] = factor * comp[c] * (1.0 if c == d else 0.25)
         return carry
 
-    lax.fori_loop(H, H + cx + 1, coupling, 0, unroll=3)
-
-    def rate(phase):
-        t = [t_s[phase, H - 1 + s] for s in range(cx + 2)]
-        ts = [a[0:cy] for a in t]
-        dz = [zhigh(a) - zlow(a) for a in t]
-        dy = [(yhigh(a) - ylow(a))[0:cy] for a in t]
+    coupling(H - 1, 0)
+    lax.fori_loop(H, H + cx + 2, coupling, 0, unroll=2)
+
+    def rate(n, rim):
+        rows = BOTH if rim else A
+        t = {x: t_s[n, H + x] for x in range(-1 - rim, cx + 1 + rim)}
+        dz = {x: zhigh(a) - zlow(a) for x, a in t.items()}
+        dy = {x: (yhigh(a) - ylow(a))[rows] for x, a in t.items()}
+        qx = {}
+        for x in range(-rim, cx + 1 + rim):
+            qx[x] = (
+                kx_s[0, x + 1, rows] * (t[x] - t[x - 1])[rows]
+                + kx_s[1, x + 1, rows] * (dy[x - 1] + dy[x])
+                + kx_s[2, x + 1, rows] * (dz[x - 1] + dz[x])[rows]
+            )
         out = []
-        qx = []
-        for x in range(cx + 1):
-            qx.append(
-                kx_s[0, x] * (ts[x + 1] - ts[x])
-                + kx_s[1, x] * (dy[x] + dy[x + 1])
-                + kx_s[2, x] * (dz[x] + dz[x + 1])[0:cy]
+        for x in range(-rim, cx + rim):
+            a, dx, z = t[x], t[x + 1] - t[x - 1], dz[x]
+            qy = (
+                ky_s[1, x + 1] * (a - ylow(a))
+                + ky_s[0, x + 1] * (dx + ylow(dx))
+                + ky_s[2, x + 1] * (z + ylow(z))
             )
-        for x in range(cx):
-            a = t[x + 1]
-            dx = t[x + 2] - t[x]
-            qy = (
-                ky_s[1, x] * (a - ylow(a))
-                + ky_s[0, x] * (dx + ylow(dx))
-                + ky_s[2, x] * (dz[x + 1] + ylow(dz[x + 1]))
+            a, dx, y = a[rows], dx[rows], dy[x]
+            qz = (
+                kz_s[2, x + 1, rows] * (a - zlow(a))
+                + kz_s[0, x + 1, rows] * (dx + zlow(dx))
+                + kz_s[1, x + 1, rows] * (y + zlow(y))
             )
-            dxs = dx[0:cy]
-            qz = (
-                kz_s[2, x] * (ts[x + 1] - zlow(ts[x + 1]))
-                + kz_s[0, x] * (dxs + zlow(dxs))
-                + kz_s[1, x] * (dy[x + 1] + zlow(dy[x + 1]))
-            )
-            out.append(qx[x + 1] - qx[x] + (yhigh(qy) - qy)[0:cy] + (zhigh(qz) - qz))
+            total = qx[x + 1] - qx[x] + (yhigh(qy) - qy)[rows] + (zhigh(qz) - qz)
+            out.append(total * irho_s[H + x, rows])
         return jnp.stack(out)
 
     first_factor, factors = rkl_factors()
-    inner = pl.ds(H, cx)
-    base = e_s[inner, 0:cy, :]
-    irho = irho_s[inner, 0:cy, :]
-    rate0 = rate(0)
-    earlier, latest = base, base + first_factor * rate0
-    for n, (mu, nu, rest, fresh, zero) in enumerate(factors):
-        phase = n + 1
-        t = latest * irho
-        for x in range(cx):
-            pk[n, 0, x : x + 1, :] = t[x, cy - 1 : cy, :]
-            pk[n, 1, x : x + 1, :] = t[x, 0:1, :]
-        t_s[phase, inner, 0:cy, :] = t
-        copies = []
-        for k, (dx, dy) in enumerate(ring):
-            if dy == 1:
-                copies.append(remote(phase, k, pk.at[n, 0], low_row.at[n, dx + 1]))
-            elif dy == -1:
-                copies.append(remote(phase, k, pk.at[n, 1], high_row.at[n, dx + 1]))
-            else:
-                src = H + cx - 1 if dx == 1 else H
-                dst = H - 1 if dx == 1 else H + cx
-                copies.append(
-                    remote(
-                        phase, k,
-                        t_s.at[phase, src, pl.ds(0, cy)],
-                        t_s.at[phase, dst, pl.ds(0, cy)],
-                    )
-                )
-        part = mu * latest + nu * earlier + rest * base + zero * rate0
-        sent += copies
-        for copy in copies:
-            copy.wait_recv()
-        for s in range(cx + 2):
-            if s == 0:
-                d, x = 2, cx - 1
-            elif s == cx + 1:
-                d, x = 0, 0
-            else:
-                d, x = 1, s - 1
-            t_s[phase, H - 1 + s, cy : cy + 1, :] = high_row[n, d, x : x + 1, :]
-            t_s[phase, H - 1 + s, ROWS - 1 : ROWS, :] = low_row[n, d, x : x + 1, :]
-        earlier, latest = latest, part + fresh * rate(phase)
-    o_p[...] = (G - 1.0) * latest
+    inner, around = slice(H, H + cx), slice(H - 1, H + cx + 1)
+    start = t_s[0, around]
+    rate0 = rate(0, 1)
+    r_s[...] = rate0
+    t_s[1, around] = start + first_factor * rate0
+
+    mu, nu, rest, fresh, zero = factors[0]
+    second = (
+        mu * t_s[1, inner, A]
+        + (nu + rest) * t_s[0, inner, A]
+        + zero * r_s[1 : cx + 1, A]
+        + fresh * rate(1, 0)
+    )
+    for x in range(cx):
+        for n in range(2):
+            pk[0, n, x : x + 1, :] = second[x, cy - 2 + n : cy - 1 + n, :]
+            pk[1, n, x : x + 1, :] = second[x, n : n + 1, :]
+    t_s[2, inner, A] = second
+    copies = []
+    for k, (dx, dy) in enumerate(ring):
+        if dy == 1:
+            copies.append(remote(1, k, pk.at[0], low_row.at[dx + 1]))
+        elif dy == -1:
+            copies.append(remote(1, k, pk.at[1], high_row.at[dx + 1]))
+        else:
+            src = pl.ds(H + cx - 2 if dx == 1 else H, 2)
+            dst = pl.ds(H - 2 if dx == 1 else H + cx, 2)
+            copies.append(remote(1, k, t_s.at[2, src, near], t_s.at[2, dst, near]))
+    mu, nu, rest, fresh, zero = factors[1]
+    part = nu * t_s[1, around] + rest * t_s[0, around] + zero * r_s[...]
+    for copy in copies:
+        copy.wait_recv()
+    sent += copies
+    for x in range(-2, cx + 2):
+        d = 2 if x < 0 else (0 if x >= cx else 1)
+        row = x % cx
+        for n in range(2):
+            t_s[2, H + x, cy + n : cy + n + 1, :] = high_row[d, n, row : row + 1, :]
+            t_s[2, H + x, ROWS - 2 + n : ROWS - 1 + n, :] = low_row[d, n, row : row + 1, :]
+    t_s[3, around] = part + mu * t_s[2, around] + fresh * rate(2, 1)
+
+    mu, nu, rest, fresh, zero = factors[2]
+    last = (
+        mu * t_s[3, inner, A]
+        + nu * t_s[2, inner, A]
+        + rest * t_s[0, inner, A]
+        + zero * r_s[1 : cx + 1, A]
+        + fresh * rate(3, 0)
+    )
+    o_p[...] = last * o_rho[...]
     stores.append(pltpu.make_async_copy(o_p, p_out, out_sem.at[3]))
     stores[3].start()
     for copy in sent:
@@ -467,7 +472,6 @@
         wide = cx + 2 * H
         f32 = jnp.float32
         vm = lambda *shape: pltpu.VMEM(shape, f32)
-        phases = SECTIONS - 1
         spec = pl.BlockSpec(memory_space=pl.ANY)
         shapes = [jax.ShapeDtypeStruct(a.shape, f32) for a in (rho, v, p, b)]
         results = pl.pallas_call(
@@ -492,18 +496,18 @@
                 vm(3, ROWS, nz),
                 vm(wide, ROWS, nz),
                 vm(wide, ROWS, nz),
-                vm(wide, ROWS, nz),
                 vm(3, wide, ROWS, nz),
                 vm(3, wide, ROWS, nz),
-                vm(3, cx + 1, cy, nz),
-                vm(3, cx + 1, ROWS, nz),
-                vm(3, cx + 1, cy, nz),
+                vm(3, cx + 3, ROWS, nz),
+                vm(3, cx + 3, ROWS, nz),
+                vm(3, cx + 3, ROWS, nz),
                 vm(SECTIONS, wide, ROWS, nz),
-                vm(phases, 2, cx, nz),
-                vm(phases, 3, cx, nz),
-                vm(phases, 3, cx, nz),
-                pltpu.SemaphoreType.DMA((SECTIONS, 8)),
-                pltpu.SemaphoreType.DMA((SECTIONS, 8)),
+                vm(cx + 2, ROWS, nz),
+                vm(2, 2, cx, nz),
+                vm(3, 2, cx, nz),
+                vm(3, 2, cx, nz),
+                pltpu.SemaphoreType.DMA((2, 8)),
+                pltpu.SemaphoreType.DMA((2, 8)),
                 pltpu.SemaphoreType.DMA((4,)),
                 pltpu.SemaphoreType.DMA((4,)),
             ],

time: 35.8 us -> 30 us (0.84)
  Pallas kernels: 34.9 us -> 29.1 us
    pallas_call x1, Pallas kernels: 33.2 us -> 27.4 us  [local(): pl.pallas_call(functools.partial(kernel, nx, ny), out_shape=shapes, in_sp...]
where the time goes in v4:
time: 30 us; the launch traced here: 29.8 us
  Pallas kernels  29.1 us (97%)
  between operations  0.64 us (2%)
    pallas_call x1, Pallas kernels, local(): pl.pallas_call(functools.partial(kernel, nx, ny), out_shape=shapes, in_sp...  27.4 us
    pallas_call x1, Pallas kernels, local(): pl.pallas_call(hand_on, out_shape=shapes, in_specs=[spec] * 4, out_specs=...  1.69 us

profile of v4, /device:TPU:0, one launch (start us, length us, event | category | flops | bytes accessed | tf_op | source)
XLA Modules:
  0.0 29.8 jit_solution(11375335464237269724)
XLA Ops:
  0.6 27.4 %shard_map.75 = (f32[8,8,128]{2,1,0:T(8,128)}, f32[3,8,8,128]{3,2,1,0:T(8,128)}, f32[8,8,128]{2,1,0:T(8,128)}, f32[3,8,8,128]{3,2,1,0:T(8,128)}) custom-call(f32[8,8,128]{2,1,0:T(8,128)} %rho_ref.1, f32[3,8,8,128]{3,2,1,0:T(8,128)} %v_ref.1, f32[8,8,128]{2,1,0:T(8,128)} %p_ref.1, f32[3,8,8,128]{3,2,1,0:T(8,128)} %b_ref.1), custom_call_target="tpu_custom_call" | custom-call | tf_op jit(solution)/shard_map/pallas_call | solution.py:477
  28.1 1.7 %shard_map.76 = (f32[8,8,128]{2,1,0:T(8,128)}, f32[3,8,8,128]{3,2,1,0:T(8,128)}, f32[8,8,128]{2,1,0:T(8,128)}, f32[3,8,8,128]{3,2,1,0:T(8,128)}) custom-call(f32[8,8,128]{2,1,0:T(8,128)} %get-tuple-element.8.refs_0_, f32[3,8,8,128]{3,2,1,0:T(8,128)} %get-tuple-element.9.refs_1_, f32[8,8,128]{2,1,0:T(8,128)} %get-tuple-element.10.refs_2_, ...), custom_call_target="tpu_custom_call" | custom-call | tf_op jit(solution)/shard_map/pallas_call | solution.py:516

commit v5 on v4

--- a/solution.py
+++ b/solution.py
@@ -228,12 +228,12 @@
         return k + 1 + (cx - 1) * ((k + cx - H) // (cx - 1))
 
     cells_own(H, H + cx - 1)
-    loop(cx - 1, lambda k: flux_z(H + k, A), cx - 1)
+    loop(cx - 1, lambda k: flux_z(H + k, A), 1)
     for copy in slabs:
         copy.wait_recv()
     cells_own(0, H)
     cells_own(H + cx - 1, wide - 1)
-    loop(cx - 1, lambda k: flux_z(outer(k), A), cx - 1)
+    loop(cx - 1, lambda k: flux_z(outer(k), A), 1)
     loop(cx + 4, lambda k: flux_x(2 + k, A), 2)
 
     corners = []
@@ -257,7 +257,7 @@
         flux_z(H + k, B)
 
     loop(cx - 1, middle, 1)
-    loop(cx - 3, lambda k: flux_x(H + 2 + k, B), cx - 3)
+    loop(cx - 3, lambda k: flux_x(H + 2 + k, B), 1)
 
     for copy in corners:
         copy.wait_recv()
@@ -511,7 +511,9 @@
                 pltpu.SemaphoreType.DMA((4,)),
                 pltpu.SemaphoreType.DMA((4,)),
             ],
-            compiler_params=pltpu.CompilerParams(collective_id=0, has_side_effects=True),
+            compiler_params=pltpu.CompilerParams(
+                collective_id=0, has_side_effects=True, vmem_limit_bytes=16 << 20
+            ),
         )(rho, v, p, b)
         return pl.pallas_call(
             hand_on,
@@ -520,6 +522,7 @@
             out_specs=[spec] * 4,
             scratch_shapes=[vm(*a.shape) for a in shapes]
             + [pltpu.SemaphoreType.DMA((4,)), pltpu.SemaphoreType.DMA((4,))],
+            compiler_params=pltpu.CompilerParams(vmem_limit_bytes=16 << 20),
         )(*results)
 
     placed = (

time: 30 us -> 32.6 us (1.087)
  local copies, waits for them, and re-layouts: 0 us -> 3.29 us
  Pallas kernels: 29.1 us -> 28.3 us
    unnamed x0 -> x8, local copies, waits for them, and re-layouts: none -> 3.29 us
    pallas_call x1, Pallas kernels: 1.69 us -> 1.1 us  [local(): pl.pallas_call(hand_on, out_shape=shapes, in_specs=[spec] * 4, out_specs=...]
where the time goes in v5:
time: 32.6 us; the launch traced here: 32.3 us
  Pallas kernels  28.3 us (87%)
  local copies, waits for them, and re-layouts  3.29 us (10%)
  between operations  0.65 us (2%)
    pallas_call x1, Pallas kernels, local(): pl.pallas_call(functools.partial(kernel, nx, ny), out_shape=shapes, in_sp...  27.2 us
    unnamed x8, local copies, waits for them, and re-layouts  3.29 us
    pallas_call x1, Pallas kernels, local(): pl.pallas_call(hand_on, out_shape=shapes, in_specs=[spec] * 4, out_specs=...  1.1 us

profile of v5, /device:TPU:0, one launch (start us, length us, event | category | flops | bytes accessed | tf_op | source)
XLA Modules:
  0.0 32.3 jit_solution(4676750046581622483)
XLA Ops:
  0.6 0.0 copy-start
  0.6 0.9 %copy-done = f32[3,8,8,128]{3,2,1,0:T(8,128)S(1)} copy-done((f32[3,8,8,128]{3,2,1,0:T(8,128)S(1)}, f32[3,8,8,128]{3,2,1,0:T(8,128)}, u32[]{:S(2)}) %copy-start) | copy-done | bytes 98328
  1.5 0.0 copy-start.1
  1.5 0.9 %copy-done.1 = f32[3,8,8,128]{3,2,1,0:T(8,128)S(1)} copy-done((f32[3,8,8,128]{3,2,1,0:T(8,128)S(1)}, f32[3,8,8,128]{3,2,1,0:T(8,128)}, u32[]{:S(2)}) %copy-start.1) | copy-done | bytes 98328
  2.4 0.0 copy-start.2
  2.4 0.8 %copy-done.2 = f32[8,8,128]{2,1,0:T(8,128)S(1)} copy-done((f32[8,8,128]{2,1,0:T(8,128)S(1)}, f32[8,8,128]{2,1,0:T(8,128)}, u32[]{:S(2)}) %copy-start.2) | copy-done | bytes 32792
  3.2 0.0 copy-start.3
  3.2 0.8 %copy-done.3 = f32[8,8,128]{2,1,0:T(8,128)S(1)} copy-done((f32[8,8,128]{2,1,0:T(8,128)S(1)}, f32[8,8,128]{2,1,0:T(8,128)}, u32[]{:S(2)}) %copy-start.3) | copy-done | bytes 32792
  3.9 27.2 %shard_map.75 = (f32[8,8,128]{2,1,0:T(8,128)S(1)}, f32[3,8,8,128]{3,2,1,0:T(8,128)S(1)}, f32[8,8,128]{2,1,0:T(8,128)S(1)}, f32[3,8,8,128]{3,2,1,0:T(8,128)S(1)}) custom-call(f32[8,8,128]{2,1,0:T(8,128)S(1)} %copy-done.2, f32[3,8,8,128]{3,2,1,0:T(8,128)S(1)} %copy-done, f32[8,8,128]{2,1,0:T(8,128)S(1)} %copy-done.3, f32[3,8,8,128]{3,2,1,0:T(8,128)S(1)} %copy-done.1), custom_call_target="tpu_custom_call" | custom-call | tf_op jit(solution)/shard_map/pallas_call | solution.py:477
  31.2 1.1 %shard_map.76 = (f32[8,8,128]{2,1,0:T(8,128)}, f32[3,8,8,128]{3,2,1,0:T(8,128)}, f32[8,8,128]{2,1,0:T(8,128)}, f32[3,8,8,128]{3,2,1,0:T(8,128)}) custom-call(f32[8,8,128]{2,1,0:T(8,128)S(1)} %get-tuple-element.8.refs_0_, f32[3,8,8,128]{3,2,1,0:T(8,128)S(1)} %get-tuple-element.9.refs_1_, f32[8,8,128]{2,1,0:T(8,128)S(1)} %get-tuple-element.10.refs_2_, ...), custom_call_target="tpu_custom_call" | custom-call | tf_op jit(solution)/shard_map/pallas_call | solution.py:518
Async XLA Ops:
  0.6 0.9 %copy-start = (f32[3,8,8,128]{3,2,1,0:T(8,128)S(1)}, f32[3,8,8,128]{3,2,1,0:T(8,128)}, u32[]{:S(2)}) copy-start(f32[3,8,8,128]{3,2,1,0:T(8,128)} %v_ref.1) | copy-start | bytes 294916
  1.5 0.9 %copy-start.1 = (f32[3,8,8,128]{3,2,1,0:T(8,128)S(1)}, f32[3,8,8,128]{3,2,1,0:T(8,128)}, u32[]{:S(2)}) copy-start(f32[3,8,8,128]{3,2,1,0:T(8,128)} %b_ref.1) | copy-start | bytes 294916
  2.4 0.8 %copy-start.2 = (f32[8,8,128]{2,1,0:T(8,128)S(1)}, f32[8,8,128]{2,1,0:T(8,128)}, u32[]{:S(2)}) copy-start(f32[8,8,128]{2,1,0:T(8,128)} %rho_ref.1) | copy-start | bytes 98308
  3.2 0.8 %copy-start.3 = (f32[8,8,128]{2,1,0:T(8,128)S(1)}, f32[8,8,128]{2,1,0:T(8,128)}, u32[]{:S(2)}) copy-start(f32[8,8,128]{2,1,0:T(8,128)} %p_ref.1) | copy-start | bytes 98308

commit v6 on v4

--- a/solution.py
+++ b/solution.py
@@ -234,7 +234,7 @@
     cells_own(0, H)
     cells_own(H + cx - 1, wide - 1)
     loop(cx - 1, lambda k: flux_z(outer(k), A), cx - 1)
-    loop(cx + 4, lambda k: flux_x(2 + k, A), 2)
+    loop(cx + 4, lambda k: flux_x(2 + k, A), 4)
 
     corners = []
     for copy, dy, buffer in ((to_high, 1, from_low), (to_low, -1, from_high)):
@@ -256,7 +256,7 @@
         flux_y(H + k)
         flux_z(H + k, B)
 
-    loop(cx - 1, middle, 1)
+    loop(cx - 1, middle, cx - 1)
     loop(cx - 3, lambda k: flux_x(H + 2 + k, B), cx - 3)
 
     for copy in corners:
@@ -273,8 +273,8 @@
         flux_y(outer(k))
         flux_z(outer(k), B)
 
-    loop(cx - 1, ends, 1)
-    loop(2 * H, lambda k: flux_x(2 + k + (cx - 3) * (k // H), B), 2)
+    loop(cx - 1, ends, cx - 1)
+    loop(2 * H, lambda k: flux_x(2 + k + (cx - 3) * (k // H), B), H)
     flux_x(wide - 2, A)
 
     def body(i):
@@ -332,7 +332,7 @@
             o_b[c, x] = a[A]
 
     body(2)
-    loop(cx + 2, lambda k: body(3 + k), 2)
+    loop(cx + 2, lambda k: body(3 + k), 5)
     body(wide - 3)
     body(wide - 2)
     stores = [
@@ -360,7 +360,7 @@
         return carry
 
     coupling(H - 1, 0)
-    lax.fori_loop(H, H + cx + 2, coupling, 0, unroll=2)
+    lax.fori_loop(H, H + cx + 2, coupling, 0, unroll=5)
 
     def rate(n, rim):
         rows = BOTH if rim else A

time: 30 us -> 28.3 us (0.943)
  Pallas kernels: 29.1 us -> 27.5 us
    pallas_call x1, Pallas kernels: 27.4 us -> 25.8 us  [local(): pl.pallas_call(functools.partial(kernel, nx, ny), out_shape=shapes, in_sp...]
where the time goes in v6:
time: 28.3 us; the launch traced here: 28.1 us
  Pallas kernels  27.5 us (97%)
  between operations  0.64 us (2%)
    pallas_call x1, Pallas kernels, local(): pl.pallas_call(functools.partial(kernel, nx, ny), out_shape=shapes, in_sp...  25.8 us
    pallas_call x1, Pallas kernels, local(): pl.pallas_call(hand_on, out_shape=shapes, in_specs=[spec] * 4, out_specs=...  1.69 us

profile of v6, /device:TPU:0, one launch (start us, length us, event | category | flops | bytes accessed | tf_op | source)
XLA Modules:
  0.0 28.1 jit_solution(2312201307264815636)
XLA Ops:
  0.6 25.8 %shard_map.75 = (f32[8,8,128]{2,1,0:T(8,128)}, f32[3,8,8,128]{3,2,1,0:T(8,128)}, f32[8,8,128]{2,1,0:T(8,128)}, f32[3,8,8,128]{3,2,1,0:T(8,128)}) custom-call(f32[8,8,128]{2,1,0:T(8,128)} %rho_ref.1, f32[3,8,8,128]{3,2,1,0:T(8,128)} %v_ref.1, f32[8,8,128]{2,1,0:T(8,128)} %p_ref.1, f32[3,8,8,128]{3,2,1,0:T(8,128)} %b_ref.1), custom_call_target="tpu_custom_call" | custom-call | tf_op jit(solution)/shard_map/pallas_call | solution.py:477
  26.4 1.7 %shard_map.76 = (f32[8,8,128]{2,1,0:T(8,128)}, f32[3,8,8,128]{3,2,1,0:T(8,128)}, f32[8,8,128]{2,1,0:T(8,128)}, f32[3,8,8,128]{3,2,1,0:T(8,128)}) custom-call(f32[8,8,128]{2,1,0:T(8,128)} %get-tuple-element.8.refs_0_, f32[3,8,8,128]{3,2,1,0:T(8,128)} %get-tuple-element.9.refs_1_, f32[8,8,128]{2,1,0:T(8,128)} %get-tuple-element.10.refs_2_, ...), custom_call_target="tpu_custom_call" | custom-call | tf_op jit(solution)/shard_map/pallas_call | solution.py:516

commit v7 on v6

--- a/solution.py
+++ b/solution.py
@@ -234,7 +234,7 @@
     cells_own(0, H)
     cells_own(H + cx - 1, wide - 1)
     loop(cx - 1, lambda k: flux_z(outer(k), A), cx - 1)
-    loop(cx + 4, lambda k: flux_x(2 + k, A), 4)
+    loop(cx + 4, lambda k: flux_x(2 + k, A), 6)
 
     corners = []
     for copy, dy, buffer in ((to_high, 1, from_low), (to_low, -1, from_high)):
@@ -274,7 +274,7 @@
         flux_z(outer(k), B)
 
     loop(cx - 1, ends, cx - 1)
-    loop(2 * H, lambda k: flux_x(2 + k + (cx - 3) * (k // H), B), H)
+    loop(2 * H, lambda k: flux_x(2 + k + (cx - 3) * (k // H), B), 2 * H)
     flux_x(wide - 2, A)
 
     def body(i):
@@ -332,7 +332,7 @@
             o_b[c, x] = a[A]
 
     body(2)
-    loop(cx + 2, lambda k: body(3 + k), 5)
+    loop(cx + 2, lambda k: body(3 + k), 10)
     body(wide - 3)
     body(wide - 2)
     stores = [
@@ -360,7 +360,7 @@
         return carry
 
     coupling(H - 1, 0)
-    lax.fori_loop(H, H + cx + 2, coupling, 0, unroll=5)
+    lax.fori_loop(H, H + cx + 2, coupling, 0, unroll=10)
 
     def rate(n, rim):
         rows = BOTH if rim else A

time: 28.3 us -> 28.5 us (level)
  no operation moved by 1% of the time
where the time goes in v7:
time: 28.5 us; the launch traced here: 28.3 us
  Pallas kernels  27.6 us (97%)
  between operations  0.64 us (2%)
    pallas_call x1, Pallas kernels, local(): pl.pallas_call(functools.partial(kernel, nx, ny), out_shape=shapes, in_sp...  25.9 us
    pallas_call x1, Pallas kernels, local(): pl.pallas_call(hand_on, out_shape=shapes, in_specs=[spec] * 4, out_specs=...  1.69 us

profile of v7, /device:TPU:0, one launch (start us, length us, event | category | flops | bytes accessed | tf_op | source)
XLA Modules:
  0.0 28.3 jit_solution(10780222385986428796)
XLA Ops:
  0.6 25.9 %shard_map.75 = (f32[8,8,128]{2,1,0:T(8,128)}, f32[3,8,8,128]{3,2,1,0:T(8,128)}, f32[8,8,128]{2,1,0:T(8,128)}, f32[3,8,8,128]{3,2,1,0:T(8,128)}) custom-call(f32[8,8,128]{2,1,0:T(8,128)} %rho_ref.1, f32[3,8,8,128]{3,2,1,0:T(8,128)} %v_ref.1, f32[8,8,128]{2,1,0:T(8,128)} %p_ref.1, f32[3,8,8,128]{3,2,1,0:T(8,128)} %b_ref.1), custom_call_target="tpu_custom_call" | custom-call | tf_op jit(solution)/shard_map/pallas_call | solution.py:477
  26.6 1.7 %shard_map.76 = (f32[8,8,128]{2,1,0:T(8,128)}, f32[3,8,8,128]{3,2,1,0:T(8,128)}, f32[8,8,128]{2,1,0:T(8,128)}, f32[3,8,8,128]{3,2,1,0:T(8,128)}) custom-call(f32[8,8,128]{2,1,0:T(8,128)} %get-tuple-element.8.refs_0_, f32[3,8,8,128]{3,2,1,0:T(8,128)} %get-tuple-element.9.refs_1_, f32[8,8,128]{2,1,0:T(8,128)} %get-tuple-element.10.refs_2_, ...), custom_call_target="tpu_custom_call" | custom-call | tf_op jit(solution)/shard_map/pallas_call | solution.py:516
